TPU v7x, 32 devices: a whole 2x2x4 slice. The times are simulated.
32 devices in a mesh: stream: 4 (over x, core), items: 8 (over z, y).
Axes of the slice: x: 2, y: 2, z: 4, core: 2. Of those that a mesh axis runs over, the one named last changes fastest.
Arguments:
- tokens: bfloat16 [32, 264, 768], P('items', 'stream'), may hold values from -6 to 6
- cotangent: bfloat16 [32, 264, 768], P('items', 'stream'), may hold values from -6 to 6
- text_len: int32 [32], P('items'), may hold values from 4 to 40, as said below
- attn_in: bfloat16 [2, 768, 2304], replicated, may hold values from -0.21875 to 0.21875
- attn_bias: bfloat16 [2, 2, 768], replicated, may hold values from -3 to 3
- attn_out: bfloat16 [2, 768, 768], replicated, may hold values from -0.875 to 0.875
- out_bias: bfloat16 [2, 768], replicated, may hold values from -3 to 3
- norm_gain: bfloat16 [2, 2, 768], replicated, may hold values from 0.25 to 1.75
- norm_bias: bfloat16 [2, 2, 768], replicated, may hold values from -2 to 2
- ffn_in: bfloat16 [3, 768, 3072], replicated, may hold values from -0.21875 to 0.21875
- ffn_in_bias: bfloat16 [3, 3072], replicated, may hold values from -2 to 2
- ffn_out: bfloat16 [3, 3072, 768], replicated, may hold values from -0.109375 to 0.109375
- ffn_out_bias: bfloat16 [3, 768], replicated, may hold values from -2 to 2
Outputs:
- mixed: bfloat16 [32, 264, 768], P('items', 'stream')
- tokens_grad: float32 [32, 264, 768], P('items', 'stream')
- attn_in_grad: float32 [2, 768, 2304], P(None, 'items')
- attn_bias_grad: float32 [2, 2, 768], P(None, None, 'items')
- attn_out_grad: float32 [2, 768, 768], P(None, 'items')
- out_bias_grad: float32 [2, 768], P(None, 'items')
- norm_gain_grad: float32 [2, 2, 768], P(None, None, 'items')
- norm_bias_grad: float32 [2, 2, 768], P(None, None, 'items')
- ffn_in_grad: float32 [3, 768, 3072], P(None, 'items')
- ffn_in_bias_grad: float32 [3, 3072], P(None, 'items')
- ffn_out_grad: float32 [3, 3072, 768], P(None, 'items')
- ffn_out_bias_grad: float32 [3, 768], P(None, 'items')
Inputs may be any that keep to these rules, and one draw needn't show every extreme that they name: `text_len`: one item of every draw has exactly 40 text tokens.
All inputs are finite; a program needn't handle non-finite values.
Results may differ from a plain program's by a relative error of at most 0.014.
Values may be sent and summed in bfloat16 or wider, within the bound.
No kernel may reach another device: no remote copies, remote signals or barrier semaphores. Data moves between devices by JAX's collectives and lax.ppermute only.
A program may use at most 320 MiB of HBM per device.

v0:
```python
import jax
import jax.numpy as jnp
from jax import lax
from jax.sharding import PartitionSpec as P

HEADS = 12
PATCHES = 197


norm_eps = 1e-06
masked_fill = -1e30


def gelu_exact(values):
    return 0.5 * values * (1.0 + lax.erf(values * 0.7071067811865476))


def gelu_slope(values):
    cumulative = 0.5 * (1.0 + lax.erf(values * 0.7071067811865476))
    density = jnp.exp(-0.5 * values * values) * 0.3989422804014327
    return cumulative + values * density


def norm_forward(values, gain, offset):
    row_mean = jnp.mean(values, axis=-1, keepdims=True)
    centred = values - row_mean
    row_var = jnp.mean(centred * centred, axis=-1, keepdims=True)
    inv_std = lax.rsqrt(row_var + norm_eps)
    scaled = centred * inv_std
    return (scaled * gain + offset, scaled, inv_std)


def norm_backward(grad_out, scaled, inv_std, gain):
    grad_scaled = grad_out * gain
    mean_first = jnp.mean(grad_scaled, axis=-1, keepdims=True)
    mean_second = jnp.mean(grad_scaled * scaled, axis=-1, keepdims=True)
    grad_in = inv_std * (grad_scaled - mean_first - scaled * mean_second)
    return (grad_in, jnp.sum(grad_out * scaled, axis=(0, 1)), jnp.sum(grad_out, axis=(0, 1)))


def project(left, right):
    return jnp.einsum("isd,df->isf", left, right, preferred_element_type=jnp.float32)


def project_back(left, right):
    return jnp.einsum("isf,df->isd", left, right, preferred_element_type=jnp.float32)


def weight_grad(left, right):
    return jnp.einsum("isd,isf->df", left, right, preferred_element_type=jnp.float32)


def split_heads(values, head_count):
    return values.reshape(
        values.shape[0], values.shape[1], head_count, values.shape[2] // head_count
    )


def merge_heads(values):
    return values.reshape(values.shape[0], values.shape[1], values.shape[2] * values.shape[3])


def masked_scores(queries, keys_full, key_valid, head_count):
    query_heads = split_heads(queries, head_count)
    key_heads = split_heads(keys_full, head_count)
    score_scale = query_heads.shape[3] ** (-0.5)
    raw_scores = (
        jnp.einsum("iqhd,ikhd->ihqk", query_heads, key_heads, preferred_element_type=jnp.float32)
        * score_scale
    )
    return jnp.where(key_valid[:, None, None, :], raw_scores, masked_fill)


def split_expert(piece, is_text):
    zeroes = jnp.zeros_like(piece)
    return jnp.stack([jnp.where(is_text, zeroes, piece), jnp.where(is_text, piece, zeroes)])


def per_device(
    tokens,
    cotangent,
    text_len,
    attn_in,
    attn_bias,
    attn_out,
    out_bias,
    norm_gain,
    norm_bias,
    ffn_in,
    ffn_in_bias,
    ffn_out,
    ffn_out_bias,
):
    item_count, slot_count, width = tokens.shape
    head_count = HEADS
    stream_size = lax.axis_size("stream")
    stream_idx = lax.axis_index("stream")
    is_text = stream_idx == stream_size - 1
    positions = jnp.arange(stream_size, dtype=jnp.int32)
    patch_counts = jnp.clip(PATCHES - positions * slot_count, 0, slot_count)
    counts_all = jnp.where(
        positions[None, :] == stream_size - 1, text_len[:, None], patch_counts[None, :]
    )
    slot_place = jnp.arange(slot_count, dtype=jnp.int32)
    key_valid = (slot_place[None, None, :] < counts_all[:, :, None]).reshape(
        item_count, stream_size * slot_count
    )
    own_patch = jnp.clip(PATCHES - stream_idx * slot_count, 0, slot_count)
    own_count = jnp.where(is_text, text_len, own_patch)
    row_valid = (slot_place[None, :] < own_count[:, None]).astype(jnp.float32)[:, :, None]
    expert_ids = (jnp.where(is_text, 1, 0), 2)
    state = tokens.astype(jnp.float32)
    saved = []
    for layer_no in range(2):
        gain_rows = norm_gain[layer_no].astype(jnp.float32)
        offset_rows = norm_bias[layer_no].astype(jnp.float32)
        normed, scaled_one, inv_one = norm_forward(state, gain_rows[0], offset_rows[0])
        normed_low = normed.astype(jnp.bfloat16)
        packed = project(normed_low, attn_in[layer_no])
        bias_rows = attn_bias[layer_no].astype(jnp.float32)
        queries = (packed[:, :, :width] + bias_rows[0]).astype(jnp.bfloat16)
        keys_own = packed[:, :, width : 2 * width].astype(jnp.bfloat16)
        values_own = (packed[:, :, 2 * width :] + bias_rows[1]).astype(jnp.bfloat16)
        keys_full, values_full = (
            lax.all_gather(keys_own, "stream", axis=1, tiled=True),
            lax.all_gather(values_own, "stream", axis=1, tiled=True),
        )
        scores = masked_scores(queries, keys_full, key_valid, head_count)
        row_max = jnp.max(scores, axis=-1, keepdims=True)
        exponent = jnp.exp(scores - row_max)
        row_total = jnp.sum(exponent, axis=-1, keepdims=True)
        softmaxed = (exponent / row_total).astype(jnp.bfloat16)
        context = merge_heads(
            jnp.einsum(
                "ihqk,ikhd->iqhd",
                softmaxed,
                split_heads(values_full, head_count),
                preferred_element_type=jnp.float32,
            )
        ).astype(jnp.bfloat16)
        state = state + (
            project(context, attn_out[layer_no]) + out_bias[layer_no].astype(jnp.float32)
        )
        normed_two, scaled_two, inv_two = norm_forward(state, gain_rows[1], offset_rows[1])
        normed_two_low = normed_two.astype(jnp.bfloat16)
        expert = expert_ids[layer_no]
        weight_in = lax.dynamic_index_in_dim(ffn_in, expert, 0, keepdims=False)
        weight_out = lax.dynamic_index_in_dim(ffn_out, expert, 0, keepdims=False)
        bias_in = lax.dynamic_index_in_dim(ffn_in_bias, expert, 0, keepdims=False).astype(
            jnp.float32
        )
        bias_out = lax.dynamic_index_in_dim(ffn_out_bias, expert, 0, keepdims=False).astype(
            jnp.float32
        )
        pre_act = project(normed_two_low, weight_in) + bias_in
        activated = gelu_exact(pre_act).astype(jnp.bfloat16)
        state = state + (project(activated, weight_out) + bias_out)
        saved.append(
            (
                normed_low,
                scaled_one,
                inv_one,
                queries,
                keys_own,
                values_own,
                keys_full,
                values_full,
                row_max,
                row_total,
                context,
                normed_two_low,
                scaled_two,
                inv_two,
                pre_act,
                activated,
                weight_in,
                weight_out,
            )
        )
    mixed = state.astype(jnp.bfloat16)
    grad_state = cotangent.astype(jnp.float32) * row_valid
    layer_sums = [None, None]
    for layer_no in (1, 0):
        (
            normed_low,
            scaled_one,
            inv_one,
            queries,
            keys_own,
            values_own,
            keys_full,
            values_full,
            row_max,
            row_total,
            context,
            normed_two_low,
            scaled_two,
            inv_two,
            pre_act,
            activated,
            weight_in,
            weight_out,
        ) = saved[layer_no]
        gain_rows = norm_gain[layer_no].astype(jnp.float32)
        grad_branch = grad_state.astype(jnp.bfloat16)
        grad_ffn_out = weight_grad(activated, grad_branch)
        grad_ffn_out_bias = jnp.sum(grad_branch.astype(jnp.float32), axis=(0, 1))
        grad_act = project_back(grad_branch, weight_out)
        grad_pre = (grad_act * gelu_slope(pre_act)).astype(jnp.bfloat16)
        grad_ffn_in = weight_grad(normed_two_low, grad_pre)
        grad_ffn_in_bias = jnp.sum(grad_pre.astype(jnp.float32), axis=(0, 1))
        grad_normed = project_back(grad_pre, weight_in)
        grad_in, grad_gain_two, grad_offset_two = norm_backward(
            grad_normed, scaled_two, inv_two, gain_rows[1]
        )
        grad_state = grad_state + grad_in
        grad_branch = grad_state.astype(jnp.bfloat16)
        grad_attn_out = weight_grad(context, grad_branch)
        grad_out_bias = jnp.sum(grad_branch.astype(jnp.float32), axis=(0, 1))
        grad_context = project_back(grad_branch, attn_out[layer_no]).astype(jnp.bfloat16)
        scores = masked_scores(queries, keys_full, key_valid, head_count)
        probs_full = jnp.exp(scores - row_max) / row_total
        context_heads = split_heads(grad_context, head_count)
        query_heads = split_heads(queries, head_count)
        key_heads = split_heads(keys_full, head_count)
        value_heads = split_heads(values_full, head_count)
        score_scale = query_heads.shape[3] ** (-0.5)
        grad_probs = jnp.einsum(
            "iqhd,ikhd->ihqk", context_heads, value_heads, preferred_element_type=jnp.float32
        )
        partial_values = merge_heads(
            jnp.einsum(
                "ihqk,iqhd->ikhd",
                probs_full.astype(jnp.bfloat16),
                context_heads,
                preferred_element_type=jnp.float32,
            )
        )
        inner_sum = jnp.sum(probs_full * grad_probs, axis=-1, keepdims=True)
        grad_scores = (probs_full * (grad_probs - inner_sum)).astype(jnp.bfloat16)
        grad_queries = (
            merge_heads(
                jnp.einsum(
                    "ihqk,ikhd->iqhd", grad_scores, key_heads, preferred_element_type=jnp.float32
                )
            )
            * score_scale
        ).astype(jnp.bfloat16)
        partial_keys = (
            merge_heads(
                jnp.einsum(
                    "ihqk,iqhd->ikhd", grad_scores, query_heads, preferred_element_type=jnp.float32
                )
            )
            * score_scale
        )
        grad_keys, grad_values = (
            lax.psum_scatter(
                partial_keys.astype(jnp.bfloat16), "stream", scatter_dimension=1, tiled=True
            ).astype(jnp.float32),
            lax.psum_scatter(
                partial_values.astype(jnp.bfloat16), "stream", scatter_dimension=1, tiled=True
            ).astype(jnp.float32),
        )
        grad_packed = jnp.concatenate(
            [grad_queries, grad_keys.astype(jnp.bfloat16), grad_values.astype(jnp.bfloat16)],
            axis=-1,
        )
        grad_attn_in = weight_grad(normed_low, grad_packed)
        grad_attn_bias = jnp.stack(
            [
                jnp.sum(grad_packed[:, :, :width].astype(jnp.float32), axis=(0, 1)),
                jnp.sum(grad_packed[:, :, 2 * width :].astype(jnp.float32), axis=(0, 1)),
            ]
        )
        grad_normed = project_back(grad_packed, attn_in[layer_no])
        grad_in, grad_gain_one, grad_offset_one = norm_backward(
            grad_normed, scaled_one, inv_one, gain_rows[0]
        )
        grad_state = grad_state + grad_in
        grad_gains = jnp.stack([grad_gain_one, grad_gain_two])
        grad_offsets = jnp.stack([grad_offset_one, grad_offset_two])
        ffn_pieces = (
            grad_ffn_in[None],
            grad_ffn_in_bias[None],
            grad_ffn_out[None],
            grad_ffn_out_bias[None],
        )
        stacked_first = False
        if layer_no == 0:
            ffn_pieces = (
                split_expert(grad_ffn_in, is_text),
                split_expert(grad_ffn_in_bias, is_text),
                split_expert(grad_ffn_out, is_text),
                split_expert(grad_ffn_out_bias, is_text),
            )
            stacked_first = True
        summed = (
            lax.psum_scatter(grad_attn_in, "items", scatter_dimension=0, tiled=True),
            lax.psum_scatter(grad_attn_bias, "items", scatter_dimension=1, tiled=True),
            lax.psum_scatter(grad_attn_out, "items", scatter_dimension=0, tiled=True),
            lax.psum_scatter(grad_out_bias, "items", scatter_dimension=0, tiled=True),
            lax.psum_scatter(grad_gains, "items", scatter_dimension=1, tiled=True),
            lax.psum_scatter(grad_offsets, "items", scatter_dimension=1, tiled=True),
            lax.psum_scatter(ffn_pieces[0], "items", scatter_dimension=1, tiled=True),
            lax.psum_scatter(ffn_pieces[1], "items", scatter_dimension=1, tiled=True),
            lax.psum_scatter(ffn_pieces[2], "items", scatter_dimension=1, tiled=True),
            lax.psum_scatter(ffn_pieces[3], "items", scatter_dimension=1, tiled=True),
        )
        shares = list(summed)
        quarters = (
            lax.psum_scatter(
                shares[0].astype(jnp.bfloat16), "stream", scatter_dimension=1, tiled=True
            ).astype(jnp.float32),
            lax.psum_scatter(
                shares[2].astype(jnp.bfloat16), "stream", scatter_dimension=1, tiled=True
            ).astype(jnp.float32),
            lax.psum_scatter(
                shares[6].astype(jnp.bfloat16), "stream", scatter_dimension=2, tiled=True
            ).astype(jnp.float32),
            lax.psum_scatter(
                shares[8].astype(jnp.bfloat16), "stream", scatter_dimension=2, tiled=True
            ).astype(jnp.float32),
        )
        matrices = (
            lax.all_gather(quarters[0].astype(jnp.bfloat16), "stream", axis=1, tiled=True).astype(
                jnp.float32
            ),
            lax.all_gather(quarters[1].astype(jnp.bfloat16), "stream", axis=1, tiled=True).astype(
                jnp.float32
            ),
            lax.all_gather(quarters[2].astype(jnp.bfloat16), "stream", axis=2, tiled=True).astype(
                jnp.float32
            ),
            lax.all_gather(quarters[3].astype(jnp.bfloat16), "stream", axis=2, tiled=True).astype(
                jnp.float32
            ),
        )
        smalls = lax.psum(
            (shares[1], shares[3], shares[4], shares[5], shares[7], shares[9]), "stream"
        )
        totals = (
            matrices[0],
            smalls[0],
            matrices[1],
            smalls[1],
            smalls[2],
            smalls[3],
            matrices[2],
            smalls[4],
            matrices[3],
            smalls[5],
        )
        layer_sums[layer_no] = totals
    first_sums, second_sums = (layer_sums[0], layer_sums[1])
    attn_in_grad = jnp.stack([first_sums[0], second_sums[0]])
    attn_bias_grad = jnp.stack([first_sums[1], second_sums[1]])
    attn_out_grad = jnp.stack([first_sums[2], second_sums[2]])
    out_bias_grad = jnp.stack([first_sums[3], second_sums[3]])
    norm_gain_grad = jnp.stack([first_sums[4], second_sums[4]])
    norm_bias_grad = jnp.stack([first_sums[5], second_sums[5]])
    ffn_in_grad = jnp.concatenate([first_sums[6], second_sums[6]], axis=0)
    ffn_in_bias_grad = jnp.concatenate([first_sums[7], second_sums[7]], axis=0)
    ffn_out_grad = jnp.concatenate([first_sums[8], second_sums[8]], axis=0)
    ffn_out_bias_grad = jnp.concatenate([first_sums[9], second_sums[9]], axis=0)
    return (
        mixed,
        grad_state,
        attn_in_grad,
        attn_bias_grad,
        attn_out_grad,
        out_bias_grad,
        norm_gain_grad,
        norm_bias_grad,
        ffn_in_grad,
        ffn_in_bias_grad,
        ffn_out_grad,
        ffn_out_bias_grad,
    )


def solution(mesh):
    return jax.shard_map(
        per_device,
        mesh=mesh,
        in_specs=(
            P("items", "stream", None),
            P("items", "stream", None),
            P("items"),
            P(),
            P(),
            P(),
            P(),
            P(),
            P(),
            P(),
            P(),
            P(),
            P(),
        ),
        out_specs=(
            P("items", "stream", None),
            P("items", "stream", None),
            P(None, "items", None),
            P(None, None, "items"),
            P(None, "items", None),
            P(None, "items"),
            P(None, None, "items"),
            P(None, None, "items"),
            P(None, "items", None),
            P(None, "items"),
            P(None, "items", None),
            P(None, "items"),
        ),
        check_vma=False,
    )
```

profile of v0, /device:TPU:0, one launch (start us, length us, event | category | flops | bytes accessed | tf_op | source)
XLA Modules:
  0.0 2613.1 jit_solution(11082243754946362265)
XLA Ops:
  22.6 17.6 all-gather.11.cloned.1.call-done
  48.5 13.9 all-gather.9.cloned.1.call-done
  73.1 6.4 multiply_convert_fusion.5
  93.4 15.0 all-gather.15.cloned.1.call-done
  113.5 5.9 fusion.155
  119.5 10.9 all-gather.13.cloned.1.call-done
  193.9 63.8 %all-reduce.16.cloned.1.call-done = (bf16[4,264,768]{2,0,1:T(4,128)(2,1)}, bf16[4,264,768]{2,0,1:T(4,128)(2,1)}) async-done(((bf16[4,264,768]{2,0,1:T(4,128)(2,1)}, bf16[4,264,768]{2,0,1:T(4,128)(2,1)}), (bf16[4,264,768]{2,0,1:T(4,128)(2,1)}, bf16[4,264,768]{2,0,1:T(4,128)(2,1)})) %all-reduce.16.cloned.1.call-update) | async-done | bytes 3244048
  269.4 6.9 pad_maximum_fusion.1
  279.7 7.4 convert_reduce_fusion.1
  296.2 6.1 convolution_bitcast_fusion.2
  307.4 6.8 pad_maximum_fusion
  322.1 7.0 convolution_bitcast_fusion.1
  360.0 229.9 %reduce-scatter.72.cloned.1.call-done = f32[2,384,768]{2,1,0:T(8,128)} async-done(((f32[2,3072,768]{2,1,0:T(8,128)}), f32[2,384,768]{2,1,0:T(8,128)}) %reduce-scatter.72.cloned.1.call-update) | async-done | bytes 2359312 | tf_op jit(solution)/shard_map/reduce_scatter | solution.py:307
  625.2 37.0 %reduce-scatter.62.cloned.1.call-done = f32[96,768]{1,0:T(8,128)} async-done(((f32[768,768]{1,0:T(8,128)}), f32[96,768]{1,0:T(8,128)}) %reduce-scatter.62.cloned.1.call-update) | async-done | bytes 294928 | tf_op jit(solution)/shard_map/reduce_scatter | solution.py:301
  665.7 68.2 %reduce-scatter.60.cloned.1.call-done = f32[96,768]{1,0:T(8,128)} async-done(((f32[768,768]{1,0:T(8,128)}), f32[96,768]{1,0:T(8,128)}) %reduce-scatter.60.cloned.1.call-update) | async-done | bytes 294928 | tf_op jit(solution)/shard_map/reduce_scatter | solution.py:301
  737.4 128.3 %reduce-scatter.58.cloned.1.call-done = f32[96,2304]{1,0:T(8,128)} async-done(((f32[768,2304]{1,0:T(8,128)}), f32[96,2304]{1,0:T(8,128)}) %reduce-scatter.58.cloned.1.call-update) | async-done | bytes 884752 | tf_op jit(solution)/shard_map/reduce_scatter | solution.py:299
  869.9 312.4 %reduce-scatter.64.cloned.1.call-done = f32[2,96,3072]{2,1,0:T(8,128)} async-done(((f32[2,768,3072]{2,1,0:T(8,128)}), f32[2,96,3072]{2,1,0:T(8,128)}) %reduce-scatter.64.cloned.1.call-update) | async-done | bytes 2359312 | tf_op jit(solution)/shard_map/reduce_scatter | solution.py:305
  1185.3 163.6 %reduce-scatter.74.cloned.1.call-done = f32[1,384,768]{2,1,0:T(8,128)} async-done(((f32[1,3072,768]{2,1,0:T(8,128)}), f32[1,384,768]{2,1,0:T(8,128)}) %reduce-scatter.74.cloned.1.call-update) | async-done | bytes 1179664 | tf_op jit(solution)/shard_map/reduce_scatter | solution.py:307
  1357.9 157.2 %reduce-scatter.68.cloned.1.call-done = f32[1,96,3072]{2,1,0:T(8,128)} async-done(((f32[1,768,3072]{2,1,0:T(8,128)}), f32[1,96,3072]{2,1,0:T(8,128)}) %reduce-scatter.68.cloned.1.call-update) | async-done | bytes 1179664 | tf_op jit(solution)/shard_map/reduce_scatter | solution.py:305
  1523.0 83.6 %all-reduce.14.cloned.1.call-done = (bf16[4,264,768]{2,0,1:T(4,128)(2,1)}, bf16[4,264,768]{2,0,1:T(4,128)(2,1)}, bf16[2,384,768]{1,0,2:T(2,128)(2,1)}) async-done(((bf16[4,264,768]{2,0,1:T(4,128)(2,1)}, bf16[4,264,768]{2,0,1:T(4,128)(2,1)}, bf16[2,384,768]{1,0,2:T(2,128)(2,1)}), (bf16[4,264,768]{2,0,1:T(4,128)(2,1)}, bf16[4,264,768]{2,0,1:T(4,128)(2,1)}, ...) | async-done | bytes 4423696
  1631.1 40.1 %reduce-scatter.104.cloned.1.call-done = f32[96,1]{1,0:T(8,128)} async-done(((f32[768,1]{1,0:T(8,128)}), f32[96,1]{1,0:T(8,128)}) %reduce-scatter.104.cloned.1.call-update) | async-done | bytes 400
  1672.1 67.0 %reduce-scatter.98.cloned.1.call-done = f32[384,1]{1,0:T(8,128)} async-done(((f32[3072,1]{1,0:T(8,128)}), f32[384,1]{1,0:T(8,128)}) %reduce-scatter.98.cloned.1.call-update) | async-done | bytes 1552
  1740.1 19.8 all-reduce.7
  1760.0 42.9 %reduce-scatter.82.cloned.1.call-done = f32[96,2]{1,0:T(8,128)} async-done(((f32[768,2]{1,0:T(8,128)}), f32[96,2]{1,0:T(8,128)}) %reduce-scatter.82.cloned.1.call-update) | async-done | bytes 784
  1803.8 63.1 %reduce-scatter.102.cloned.1.call-done = f32[96,2]{1,0:T(8,128)} async-done(((f32[768,2]{1,0:T(8,128)}), f32[96,2]{1,0:T(8,128)}) %reduce-scatter.102.cloned.1.call-update) | async-done | bytes 784
  1867.8 63.1 %reduce-scatter.94.cloned.1.call-done = f32[96,2]{1,0:T(8,128)} async-done(((f32[768,2]{1,0:T(8,128)}), f32[96,2]{1,0:T(8,128)}) %reduce-scatter.94.cloned.1.call-update) | async-done | bytes 784
  1931.7 63.2 %reduce-scatter.90.cloned.1.call-done = f32[96,2]{1,0:T(8,128)} async-done(((f32[768,2]{1,0:T(8,128)}), f32[96,2]{1,0:T(8,128)}) %reduce-scatter.90.cloned.1.call-update) | async-done | bytes 784
  1995.8 66.6 %reduce-scatter.96.cloned.1.call-done = f32[384,2]{1,0:T(8,128)} async-done(((f32[3072,2]{1,0:T(8,128)}), f32[384,2]{1,0:T(8,128)}) %reduce-scatter.96.cloned.1.call-update) | async-done | bytes 3088
  2063.4 20.1 reduce-scatter.86.cloned.1.call-done
  2089.3 16.4 reduce-scatter.84.cloned.1.call-done
  2105.7 5.8 all_gather.42
  2112.7 17.6 reduce-scatter.78.cloned.1.call-done
  2131.4 27.7 %reduce-scatter.66.cloned.1.call-done = bf16[2,96,768]{2,1,0:T(8,128)(2,1)} async-done(((bf16[2,96,3072]{2,1,0:T(8,128)(2,1)}), bf16[2,96,768]{2,1,0:T(8,128)(2,1)}) %reduce-scatter.66.cloned.1.call-update) | async-done | bytes 294928 | tf_op jit(solution)/shard_map/reduce_scatter | solution.py:318
  2159.2 6.6 all-gather.1
  2167.2 16.6 reduce-scatter.100.cloned.1.call-done
  2184.9 7.1 all_gather.47
  2193.0 15.4 reduce-scatter.70.cloned.1.call-done
  2208.4 7.6 all_gather.45
  2218.7 54.6 %reduce-scatter.80.cloned.1.call-done = f32[96,2]{1,0:T(8,128)} async-done(((f32[768,2]{1,0:T(8,128)}), f32[96,2]{1,0:T(8,128)}) %reduce-scatter.80.cloned.1.call-update) | async-done | bytes 784
  2274.2 63.2 %reduce-scatter.92.cloned.1.call-done = f32[96,2]{1,0:T(8,128)} async-done(((f32[768,2]{1,0:T(8,128)}), f32[96,2]{1,0:T(8,128)}) %reduce-scatter.92.cloned.1.call-update) | async-done | bytes 784
  2338.3 63.2 %reduce-scatter.88.cloned.1.call-done = f32[96,2]{1,0:T(8,128)} async-done(((f32[768,2]{1,0:T(8,128)}), f32[96,2]{1,0:T(8,128)}) %reduce-scatter.88.cloned.1.call-update) | async-done | bytes 784
  2402.4 10.2 all-reduce.8
  2414.3 119.7 %reduce-scatter.56.cloned.1.call-done = f32[96,2304]{1,0:T(8,128)} async-done(((f32[768,2304]{1,0:T(8,128)}), f32[96,2304]{1,0:T(8,128)}) %reduce-scatter.56.cloned.1.call-update) | async-done | bytes 884752 | tf_op jit(solution)/shard_map/reduce_scatter | solution.py:299
  2538.0 14.0 all-gather.19.cloned.1.call-done
  2557.8 6.2 copy.133
  2564.0 7.2 all-gather.17.cloned.1.call-done
  2574.4 21.7 reduce-scatter.76.cloned.1.call-done
  2597.2 6.6 all-gather
  (456 shorter events, 313.3 us)
Async XLA Ops:
  7.2 33.1 %all-gather.11.cloned.1.call-start = ((), (), s32[]{:S(2)}) async-start(), calls=%async_computation.26 | async-start | bytes 2027520 | tf_op jit(solution)/shard_map/all_gather | solution.py:125
  11.7 61.3 %copy-start.47 = (f32[768]{0:T(1024)}, f32[768]{0:T(1024)S(1)}, u32[]{:S(2)}) copy-start(f32[768]{0:T(1024)S(1)} %get-tuple-element.163) | copy-start | bytes 9220
  11.7 145.0 %copy-start.45 = (f32[768]{0:T(1024)}, f32[768]{0:T(1024)S(1)}, u32[]{:S(2)}) copy-start(f32[768]{0:T(1024)S(1)} %get-tuple-element.66) | copy-start | bytes 9220
  17.5 44.9 %all-gather.9.cloned.1.call-start = ((), (), s32[]{:S(2)}) async-start(), calls=%async_computation.25 | async-start | bytes 2027520 | tf_op jit(solution)/shard_map/all_gather | solution.py:126
  20.0 88.4 %all-gather.15.cloned.1.call-start = ((), (), s32[]{:S(2)}) async-start(), calls=%async_computation.28 | async-start | bytes 2027520 | tf_op jit(solution)/shard_map/all_gather | solution.py:125
  88.3 42.0 %all-gather.13.cloned.1.call-start = ((), (), s32[]{:S(2)}) async-start(), calls=%async_computation.27 | async-start | bytes 2027520 | tf_op jit(solution)/shard_map/all_gather | solution.py:126
  91.6 166.1 %all-reduce.16.cloned.1.call-start = ((), (), s32[]{:S(2)}) async-start(), calls=%async_computation.57 | async-start | bytes 6488064
  92.0 64.8 %copy-start.68 = (f32[4,66]{1,0:T(4,128)}, f32[4,66]{1,0:T(4,128)S(1)}, u32[]{:S(2)}) copy-start(f32[4,66]{1,0:T(4,128)S(1)} %fusion.132) | copy-start | bytes 3172
  187.3 402.5 %reduce-scatter.72.cloned.1.call-start = ((), (), s32[]{:S(2)}) async-start(), calls=%async_computation.38 | async-start | bytes 21233664 | tf_op jit(solution)/shard_map/reduce_scatter | solution.py:307
  192.3 68.6 %copy-start.7 = (f32[4,66,768]{2,1,0:T(8,128)S(1)}, f32[4,66,768]{2,1,0:T(8,128)}, u32[]{:S(2)}) copy-start(f32[4,66,768]{2,1,0:T(8,128)} %copy-done.5) | copy-start | bytes 2433028
  192.3 68.6 %copy-start.51 = (f32[768]{0:T(1024)S(1)}, f32[768]{0:T(1024)}, u32[]{:S(2)}) copy-start(f32[768]{0:T(1024)} %get-tuple-element.67) | copy-start | bytes 9220
  192.3 68.6 %copy-start.64 = (f32[4,66]{1,0:T(4,128)S(1)}, f32[4,66]{1,0:T(4,128)}, u32[]{:S(2)}) copy-start(f32[4,66]{1,0:T(4,128)} %copy-done.63) | copy-start | bytes 3172
  193.9 71.3 %copy-start.26 = (bf16[4,66,768]{2,1,0:T(8,128)(2,1)}, bf16[4,66,768]{2,1,0:T(8,128)(2,1)S(1)}, u32[]{:S(2)}) copy-start(bf16[4,66,768]{2,1,0:T(8,128)(2,1)S(1)} %copy.109) | copy-start | bytes 1216516
  276.3 386.0 %reduce-scatter.62.cloned.1.call-start = ((), (), s32[]{:S(2)}) async-start(), calls=%async_computation.32 | async-start | bytes 2654208 | tf_op jit(solution)/shard_map/reduce_scatter | solution.py:301
  279.6 454.3 %reduce-scatter.60.cloned.1.call-start = ((), (), s32[]{:S(2)}) async-start(), calls=%async_computation.31 | async-start | bytes 2654208 | tf_op jit(solution)/shard_map/reduce_scatter | solution.py:301
  296.1 569.6 %reduce-scatter.58.cloned.1.call-start = ((), (), s32[]{:S(2)}) async-start(), calls=%async_computation.30 | async-start | bytes 7962624 | tf_op jit(solution)/shard_map/reduce_scatter | solution.py:299
  302.4 880.0 %reduce-scatter.64.cloned.1.call-start = ((), (), s32[]{:S(2)}) async-start(), calls=%async_computation.33 | async-start | bytes 21233664 | tf_op jit(solution)/shard_map/reduce_scatter | solution.py:305
  314.2 1034.7 %reduce-scatter.74.cloned.1.call-start = ((), (), s32[]{:S(2)}) async-start(), calls=%async_computation.40 | async-start | bytes 10616832 | tf_op jit(solution)/shard_map/reduce_scatter | solution.py:307
  321.0 1194.1 %reduce-scatter.68.cloned.1.call-start = ((), (), s32[]{:S(2)}) async-start(), calls=%async_computation.36 | async-start | bytes 10616832 | tf_op jit(solution)/shard_map/reduce_scatter | solution.py:305
  329.1 1277.4 %all-reduce.14.cloned.1.call-start = ((), (), s32[]{:S(2)}) async-start(), calls=%async_computation.56 | async-start | bytes 8847360
  597.5 1073.8 %reduce-scatter.104.cloned.1.call-start = ((), (), s32[]{:S(2)}) async-start(), calls=%async_computation.55 | async-start | bytes 442368
  598.5 1140.6 %reduce-scatter.98.cloned.1.call-start = ((), (), s32[]{:S(2)}) async-start(), calls=%async_computation.52 | async-start | bytes 1769472
  604.1 1198.9 %reduce-scatter.82.cloned.1.call-start = ((), (), s32[]{:S(2)}) async-start(), calls=%async_computation.44 | async-start | bytes 442368
  611.0 1255.9 %reduce-scatter.102.cloned.1.call-start = ((), (), s32[]{:S(2)}) async-start(), calls=%async_computation.54 | async-start | bytes 442368
  614.6 1316.2 %reduce-scatter.94.cloned.1.call-start = ((), (), s32[]{:S(2)}) async-start(), calls=%async_computation.50 | async-start | bytes 442368
  618.3 1376.6 %reduce-scatter.90.cloned.1.call-start = ((), (), s32[]{:S(2)}) async-start(), calls=%async_computation.48 | async-start | bytes 442368
  621.3 1441.1 %reduce-scatter.96.cloned.1.call-start = ((), (), s32[]{:S(2)}) async-start(), calls=%async_computation.51 | async-start | bytes 1769472
  625.1 1458.4 %reduce-scatter.86.cloned.1.call-start = ((), (), s32[]{:S(2)}) async-start(), calls=%async_computation.46 | async-start | bytes 245760
  665.6 1440.1 %reduce-scatter.84.cloned.1.call-start = ((), (), s32[]{:S(2)}) async-start(), calls=%async_computation.45 | async-start | bytes 245760
  737.3 1393.0 %reduce-scatter.78.cloned.1.call-start = ((), (), s32[]{:S(2)}) async-start(), calls=%async_computation.42 | async-start | bytes 737280
  869.8 1289.2 %reduce-scatter.66.cloned.1.call-start = ((), (), s32[]{:S(2)}) async-start(), calls=%async_computation.34 | async-start | bytes 1474560 | tf_op jit(solution)/shard_map/reduce_scatter | solution.py:318
  1185.2 172.7 %copy-start.82 = (f32[768]{0:T(1024)S(1)}, f32[768]{0:T(1024)}, u32[]{:S(2)}) copy-start(f32[768]{0:T(1024)} %get-tuple-element.48) | copy-start | bytes 9220
  1185.2 172.7 %copy-start.81 = (f32[768]{0:T(1024)S(1)}, f32[768]{0:T(1024)}, u32[]{:S(2)}) copy-start(f32[768]{0:T(1024)} %get-tuple-element.61) | copy-start | bytes 9220
  1185.2 998.6 %reduce-scatter.100.cloned.1.call-start = ((), (), s32[]{:S(2)}) async-start(), calls=%async_computation.53 | async-start | bytes 737280
  1357.8 850.6 %reduce-scatter.70.cloned.1.call-start = ((), (), s32[]{:S(2)}) async-start(), calls=%async_computation.37 | async-start | bytes 737280 | tf_op jit(solution)/shard_map/reduce_scatter | solution.py:318
  1517.3 756.0 %reduce-scatter.80.cloned.1.call-start = ((), (), s32[]{:S(2)}) async-start(), calls=%async_computation.43 | async-start | bytes 442368
  1521.2 88.9 %copy-start.12 = (bf16[4,66,768]{2,0,1:T(4,128)(2,1)S(1)}, bf16[4,66,768]{2,0,1:T(4,128)(2,1)}, u32[]{:S(2)}) copy-start(bf16[4,66,768]{2,0,1:T(4,128)(2,1)} %param.13) | copy-start | bytes 1216516
  1521.2 88.9 %copy-start.39 = (f32[4,66]{1,0:T(4,128)S(1)}, f32[4,66]{1,0:T(4,128)}, u32[]{:S(2)}) copy-start(f32[4,66]{1,0:T(4,128)} %copy-done.38) | copy-start | bytes 3172
  1521.2 88.9 %copy-start.44 = (f32[768]{0:T(1024)S(1)}, f32[768]{0:T(1024)}, u32[]{:S(2)}) copy-start(f32[768]{0:T(1024)} %copy-done.43) | copy-start | bytes 9220
  1521.2 88.9 %copy-start.67 = (f32[4,66]{1,0:T(4,128)S(1)}, f32[4,66]{1,0:T(4,128)}, u32[]{:S(2)}) copy-start(f32[4,66]{1,0:T(4,128)} %copy-done.66) | copy-start | bytes 3172
  1614.4 723.0 %reduce-scatter.92.cloned.1.call-start = ((), (), s32[]{:S(2)}) async-start(), calls=%async_computation.49 | async-start | bytes 442368
  1615.5 786.1 %reduce-scatter.88.cloned.1.call-start = ((), (), s32[]{:S(2)}) async-start(), calls=%async_computation.47 | async-start | bytes 442368
  1616.5 917.5 %reduce-scatter.56.cloned.1.call-start = ((), (), s32[]{:S(2)}) async-start(), calls=%async_computation.29 | async-start | bytes 7962624 | tf_op jit(solution)/shard_map/reduce_scatter | solution.py:299
  1621.7 930.4 %all-gather.19.cloned.1.call-start = ((), (), s32[]{:S(2)}) async-start(), calls=%async_computation.39 | async-start | bytes 1474560 | tf_op jit(solution)/shard_map/all_gather | solution.py:335
  1624.4 946.7 %all-gather.17.cloned.1.call-start = ((), (), s32[]{:S(2)}) async-start(), calls=%async_computation.35 | async-start | bytes 1474560 | tf_op jit(solution)/shard_map/all_gather | solution.py:332
  1625.8 114.3 %copy-start.57 = (f32[768]{0:T(1024)S(1)}, f32[768]{0:T(1024)}, u32[]{:S(2)}) copy-start(f32[768]{0:T(1024)} %get-tuple-element.103) | copy-start | bytes 9220
  1625.8 114.3 %copy-start.58 = (f32[768]{0:T(1024)S(1)}, f32[768]{0:T(1024)}, u32[]{:S(2)}) copy-start(f32[768]{0:T(1024)} %get-tuple-element.101) | copy-start | bytes 9220
  2159.1 437.1 %reduce-scatter.76.cloned.1.call-start = ((), (), s32[]{:S(2)}) async-start(), calls=%async_computation.41 | async-start | bytes 737280
  (82 other events, 565.8 us)
Sparse Core Ops, SparseCore 0:
  17.6 22.6 all-gather.10
  42.4 19.9 all-gather.8
  88.4 19.9 all-gather.14
  110.4 19.9 all-gather.12
  187.5 70.2 all-reduce.15
  276.4 313.4 reduce-scatter.71
  593.9 68.2 reduce-scatter.61
  665.7 68.1 reduce-scatter.59
  737.6 128.0 reduce-scatter.57
  869.9 312.3 reduce-scatter.63
  1186.4 162.4 reduce-scatter.73
  1352.7 162.3 reduce-scatter.67
  1517.9 88.6 all-reduce.13
  1609.7 61.4 reduce-scatter.103
  1675.1 63.9 reduce-scatter.97
  1742.5 60.3 reduce-scatter.81
  1806.4 60.4 reduce-scatter.101
  1870.4 60.4 reduce-scatter.93
  1934.4 60.4 reduce-scatter.89
  1998.6 63.7 reduce-scatter.95
  2064.8 18.6 reduce-scatter.85
  2085.9 19.7 reduce-scatter.83
  2108.2 22.0 reduce-scatter.77
  2133.3 25.7 reduce-scatter.65
  2161.7 22.0 reduce-scatter.99
  2186.3 22.0 reduce-scatter.69
  2211.9 61.4 reduce-scatter.79
  2277.0 60.4 reduce-scatter.91
  2341.1 60.4 reduce-scatter.87
  2405.5 128.4 reduce-scatter.55
  2535.6 16.4 all-gather.18
  2553.7 17.4 all-gather.16
  2574.1 22.0 reduce-scatter.75
where the time goes:
time: 2630 us; the launch traced here: 2610 us
  waiting for transfers between devices  2170 us (83%)
  matrix products  146 us (6%)
  local copies, waits for them, and re-layouts  136 us (5%)
  other arithmetic  76.7 us (3%)
  blocking collectives  69.5 us (3%)
    unnamed x50, waiting for transfers between devices  827 us
    reduce_scatter x2, waiting for transfers between devices, per_device(): lax.psum_scatter(ffn_pieces[0], 'items', scatter_dimension=1, tiled=True)  470 us
    reduce_scatter x2, waiting for transfers between devices, per_device(): lax.psum_scatter(ffn_pieces[2], 'items', scatter_dimension=1, tiled=True)  393 us
    reduce_scatter x2, waiting for transfers between devices, per_device(): lax.psum_scatter(grad_attn_in, 'items', scatter_dimension=0, tiled=True)  248 us
    reduce_scatter x2, waiting for transfers between devices, per_device(): lax.psum_scatter(grad_attn_out, 'items', scatter_dimension=0, tiled=True)  105 us
    unnamed x234, local copies, waits for them, and re-layouts  66.9 us
  transfers between devices with their start and end apart: 33, of which 33 were waited for; matrix products, arithmetic and copies ran while one was open for 9% of the time, Pallas kernels for 0%

commit v1 on v0

v1 whole, which is shorter than its diff:
```python
import functools
import jax
import jax.numpy as jnp
from jax import lax
from jax.experimental import pallas as pl
from jax.experimental.pallas import tpu as pltpu
from jax.sharding import PartitionSpec as P

HEADS = 12
PATCHES = 197
TEXT = 40
F32 = jnp.float32
BF = jnp.bfloat16
EPS = 1e-06
FILL = -1e30
MIB = 1 << 20


def dot(left, right, dims=((1,), (0,))):
    return lax.dot_general(left, right, (dims, ((), ())), preferred_element_type=F32)


NT = ((1,), (1,))
TN = ((0,), (0,))


def norm_stats(values):
    row_mean = jnp.mean(values, axis=-1, keepdims=True)
    centred = values - row_mean
    row_var = jnp.mean(centred * centred, axis=-1, keepdims=True)
    inv_std = lax.rsqrt(row_var + EPS)
    return centred * inv_std, inv_std


def norm_back(grad_out, values, gain):
    scaled, inv_std = norm_stats(values)
    grad_scaled = grad_out * gain
    mean_first = jnp.mean(grad_scaled, axis=-1, keepdims=True)
    mean_second = jnp.mean(grad_scaled * scaled, axis=-1, keepdims=True)
    grad_in = inv_std * (grad_scaled - mean_first - scaled * mean_second)
    gain_sum = jnp.sum(grad_out * scaled, axis=0, keepdims=True)
    offset_sum = jnp.sum(grad_out, axis=0, keepdims=True)
    return grad_in, gain_sum, offset_sum


def gelu_parts(pre):
    cumulative = 0.5 * (1.0 + lax.erf(pre * 0.7071067811865476))
    density = jnp.exp(-0.5 * pre * pre) * 0.3989422804014327
    return pre * cumulative, cumulative + pre * density


def params(limit_mib):
    return pltpu.CompilerParams(vmem_limit_bytes=limit_mib * MIB)


def cost(flops, moved, trans=0):
    return pl.CostEstimate(flops=int(flops), bytes_accessed=int(moved), transcendentals=int(trans))


def whole(shape):
    return pl.BlockSpec(shape, lambda *_: (0,) * len(shape))


def layer_block(shape, index):
    return pl.BlockSpec((1,) + shape, lambda *_: (index,) + (0,) * len(shape))


SMEM = pl.BlockSpec(memory_space=pltpu.SMEM)


class Dims:
    def __init__(self, slots, streams, width, hidden, item_devs):
        self.slots = slots
        self.text_at = slots * (streams - 1)
        self.rows = slots * streams
        self.full = -(-self.rows // 16) * 16
        self.live = -(-(self.text_at + TEXT) // 16) * 16
        self.keys = -(-self.live // 128) * 128
        self.vis = -(-self.text_at // 16) * 16
        self.lang = self.text_at // 16 * 16
        self.width = width
        self.hidden = hidden
        self.streams = streams
        self.item_devs = item_devs
        self.share = width // item_devs


def fwd_attn_body(dm, sc, x, gain, offset, win, bias, wout, obias, n1o, qo, ko, vo, po, ctxo, x1o, n2o, n2live, ctx_s):
    width = dm.width
    xv = x[...].astype(F32)
    scaled, _ = norm_stats(xv)
    n1 = (scaled * gain[0, 0:1].astype(F32) + offset[0, 0:1].astype(F32)).astype(BF)
    n1o[...] = n1[: dm.live]
    w = win.at[0]
    q = (dot(n1, w[:, 0:width]) + bias[0, 0:1].astype(F32)).astype(BF) * 0.125
    q = q.astype(BF)
    k = dot(n1[: dm.keys], w[:, width : 2 * width]).astype(BF)
    v = (dot(n1[: dm.keys], w[:, 2 * width :]) + bias[0, 1:2].astype(F32)).astype(BF)
    qo[...] = q[: dm.live]
    ko[...] = k
    vo[...] = v
    col = lax.broadcasted_iota(jnp.int32, (1, dm.keys), 1)
    valid = (col < PATCHES) | ((col >= dm.text_at) & (col < dm.text_at + sc[0]))
    low_lane = lax.broadcasted_iota(jnp.int32, (1, 128), 1) < 64
    for pair in range(HEADS // 2):
        lanes = slice(pair * 128, pair * 128 + 128)
        qp, kp, vp = q[:, lanes], k[:, lanes], v[:, lanes]
        outs = []
        for j in range(2):
            qm = jnp.where(low_lane if j == 0 else ~low_lane, qp, jnp.zeros_like(qp))
            scores = jnp.where(valid, dot(qm, kp, NT), FILL)
            top = jnp.max(scores, axis=-1, keepdims=True)
            expo = jnp.exp(scores - top)
            probs = (expo / jnp.sum(expo, axis=-1, keepdims=True)).astype(BF)
            po[2 * pair + j] = probs[: dm.live]
            outs.append(dot(probs, vp))
        ctx_s[:, lanes] = jnp.where(low_lane, outs[0], outs[1]).astype(BF)
    ctx = ctx_s[...]
    ctxo[...] = ctx[: dm.live]
    x1 = xv + (dot(ctx, wout[0]) + obias[0].astype(F32))
    x1o[...] = x1
    scaled, _ = norm_stats(x1)
    n2 = (scaled * gain[0, 1:2].astype(F32) + offset[0, 1:2].astype(F32)).astype(BF)
    n2o[...] = n2
    n2live[...] = n2[: dm.live]


def fwd_attn(dm, layer, sc, x, norm_gain, norm_bias, attn_in, attn_bias, attn_out, out_bias):
    d, full, live, keys = dm.width, dm.full, dm.live, dm.keys
    sds = jax.ShapeDtypeStruct
    shapes = [
        sds((live, d), BF),
        sds((live, d), BF),
        sds((keys, d), BF),
        sds((keys, d), BF),
        sds((HEADS, live, keys), BF),
        sds((live, d), BF),
        sds((full, d), F32),
        sds((full, d), BF),
        sds((live, d), BF),
    ]
    return pl.pallas_call(
        functools.partial(fwd_attn_body, dm),
        grid=(1,),
        in_specs=[
            SMEM,
            whole((full, d)),
            layer_block((2, d), layer),
            layer_block((2, d), layer),
            layer_block((d, 3 * d), layer),
            layer_block((2, d), layer),
            layer_block((d, d), layer),
            layer_block((1, d), layer),
        ],
        out_specs=[whole(s.shape) for s in shapes],
        out_shape=shapes,
        scratch_shapes=[pltpu.VMEM((full, d), BF)],
        compiler_params=params(40),
        cost_estimate=cost(2 * full * d * d * 4 + 4 * full * keys * d, 8e6, HEADS * full * keys),
    )(sc, x, norm_gain, norm_bias, attn_in, attn_bias, attn_out, out_bias[:, None])


TILE = 1024


def fwd_ff_one_body(dm, last, n2, x1, wi, bi, wo, bo, slope, x2, acc):
    t = pl.program_id(0)
    act, slope_v = gelu_parts(dot(n2[...], wi[0]) + bi[0].astype(F32))
    slope[...] = slope_v[: dm.live].astype(BF)
    part = dot(act.astype(BF), wo[0])

    @pl.when(t == 0)
    def _():
        acc[...] = part + (x1[...] + bo[0].astype(F32))

    @pl.when(t > 0)
    def _():
        acc[...] += part

    @pl.when(t == pl.num_programs(0) - 1)
    def _():
        x2[...] = acc[...].astype(x2.dtype)


def fwd_ff_one(dm, expert, n2, x1, ffn_in, ffn_in_bias, ffn_out, ffn_out_bias):
    d, full, hid = dm.width, dm.full, dm.hidden
    sds = jax.ShapeDtypeStruct
    return pl.pallas_call(
        functools.partial(fwd_ff_one_body, dm, True),
        grid=(hid // TILE,),
        in_specs=[
            whole((full, d)),
            whole((full, d)),
            pl.BlockSpec((1, d, TILE), lambda t: (expert, 0, t)),
            pl.BlockSpec((1, 1, TILE), lambda t: (expert, 0, t)),
            pl.BlockSpec((1, TILE, d), lambda t: (expert, t, 0)),
            layer_block((1, d), expert),
        ],
        out_specs=[pl.BlockSpec((dm.live, TILE), lambda t: (0, t)), whole((full, d))],
        out_shape=[sds((dm.live, hid), BF), sds((full, d), BF)],
        scratch_shapes=[pltpu.VMEM((full, d), F32)],
        compiler_params=params(40),
        cost_estimate=cost(4 * full * d * hid, 12e6, 2 * full * hid),
    )(n2, x1, ffn_in, ffn_in_bias[:, None], ffn_out, ffn_out_bias[:, None])


def fwd_ff_two_body(dm, n2, x1, wv, wl, bi, wov, wol, bo, slope_v, slope_l, x2, acc):
    t = pl.program_id(0)
    vis, lang, text_at = dm.vis, dm.lang, dm.text_at
    rows_v = lax.broadcasted_iota(jnp.int32, (vis, 1), 0) < text_at
    rows_l = lax.broadcasted_iota(jnp.int32, (dm.full - lang, 1), 0) + lang >= text_at
    act_v, sv = gelu_parts(dot(n2[0:vis], wv[0]) + bi[0, 0:1].astype(F32))
    act_l, sl = gelu_parts(dot(n2[lang:], wl[0]) + bi[1, 0:1].astype(F32))
    slope_v[...] = sv.astype(BF)
    slope_l[...] = sl[: dm.live - lang].astype(BF)
    part_v = dot(act_v.astype(BF), wov[0])
    part_l = dot(act_l.astype(BF), wol[0])

    @pl.when(t == 0)
    def _():
        acc[...] = x1[...]
        part_vb = part_v + bo[0, 0:1].astype(F32)
        part_lb = part_l + bo[1, 0:1].astype(F32)
        acc[0:vis] += jnp.where(rows_v, part_vb, 0.0)
        acc[lang:] += jnp.where(rows_l, part_lb, 0.0)

    @pl.when(t > 0)
    def _():
        acc[0:vis] += jnp.where(rows_v, part_v, 0.0)
        acc[lang:] += jnp.where(rows_l, part_l, 0.0)

    @pl.when(t == pl.num_programs(0) - 1)
    def _():
        x2[...] = acc[...]


def fwd_ff_two(dm, n2, x1, ffn_in, ffn_in_bias, ffn_out, ffn_out_bias):
    d, full, hid = dm.width, dm.full, dm.hidden
    sds = jax.ShapeDtypeStruct
    count = ffn_in.shape[0]
    return pl.pallas_call(
        functools.partial(fwd_ff_two_body, dm),
        grid=(hid // TILE,),
        in_specs=[
            whole((full, d)),
            whole((full, d)),
            pl.BlockSpec((1, d, TILE), lambda t: (0, 0, t)),
            pl.BlockSpec((1, d, TILE), lambda t: (1, 0, t)),
            pl.BlockSpec((count, 1, TILE), lambda t: (0, 0, t)),
            pl.BlockSpec((1, TILE, d), lambda t: (0, t, 0)),
            pl.BlockSpec((1, TILE, d), lambda t: (1, t, 0)),
            whole((count, 1, d)),
        ],
        out_specs=[
            pl.BlockSpec((dm.vis, TILE), lambda t: (0, t)),
            pl.BlockSpec((dm.live - dm.lang, TILE), lambda t: (0, t)),
            whole((full, d)),
        ],
        out_shape=[sds((dm.vis, hid), BF), sds((dm.live - dm.lang, hid), BF), sds((full, d), F32)],
        scratch_shapes=[pltpu.VMEM((full, d), F32)],
        compiler_params=params(40),
        cost_estimate=cost(4 * full * d * hid, 21e6, 2 * full * hid),
    )(n2, x1, ffn_in, ffn_in, ffn_in_bias[:, None], ffn_out, ffn_out, ffn_out_bias[:, None])


def finish_ff_back(dm, g, gn, x1, gain, go, ga, sums):
    grad_in, gain_sum, offset_sum = norm_back(gn, x1[0 : dm.live], gain[0, 1:2].astype(F32))
    out = g[...] + grad_in
    go[...] = out
    low = out.astype(BF)
    ga[...] = low
    sums[0:1] = gain_sum
    sums[1:2] = offset_sum
    sums[2:3] = jnp.sum(low.astype(F32), axis=0, keepdims=True)


def back_ff_one_body(dm, g, gf, x1, gain, slope, wo, wi, go, ga, sums, hsum, acc):
    t = pl.program_id(0)
    gpre = (dot(gf[...], wo[0], NT) * slope[...].astype(F32)).astype(BF)
    hsum[...] = jnp.sum(gpre.astype(F32), axis=0, keepdims=True)
    part = dot(gpre, wi[0], NT)

    @pl.when(t == 0)
    def _():
        acc[...] = part

    @pl.when(t > 0)
    def _():
        acc[...] += part

    @pl.when(t == pl.num_programs(0) - 1)
    def _():
        sums[3:4] = jnp.sum(gf[...].astype(F32), axis=0, keepdims=True)
        finish_ff_back(dm, g, acc[...], x1, gain, go, ga, sums)


def back_ff_one(dm, layer, expert, g, gf, x1, norm_gain, slope, ffn_in, ffn_out):
    d, live, hid = dm.width, dm.live, dm.hidden
    sds = jax.ShapeDtypeStruct
    return pl.pallas_call(
        functools.partial(back_ff_one_body, dm),
        grid=(hid // TILE,),
        in_specs=[
            whole((live, d)),
            whole((live, d)),
            whole((dm.full, d)),
            layer_block((2, d), layer),
            pl.BlockSpec((live, TILE), lambda t: (0, t)),
            pl.BlockSpec((1, TILE, d), lambda t: (expert, t, 0)),
            pl.BlockSpec((1, d, TILE), lambda t: (expert, 0, t)),
        ],
        out_specs=[
            whole((live, d)),
            whole((live, d)),
            whole((4, d)),
            pl.BlockSpec((1, TILE), lambda t: (0, t)),
        ],
        out_shape=[sds((live, d), F32), sds((live, d), BF), sds((4, d), F32), sds((1, hid), F32)],
        scratch_shapes=[pltpu.VMEM((live, d), F32)],
        compiler_params=params(40),
        cost_estimate=cost(4 * live * d * hid, 13e6),
    )(g, gf, x1, norm_gain, slope, ffn_out, ffn_in)


def back_ff_two_body(dm, g, gf, x1, gain, slv, sll, wov, wol, wv, wl, go, ga, sums, hsum, acc):
    t = pl.program_id(0)
    vis, lang, text_at, live = dm.vis, dm.lang, dm.text_at, dm.live
    rows_v = lax.broadcasted_iota(jnp.int32, (vis, 1), 0) < text_at
    rows_l = lax.broadcasted_iota(jnp.int32, (live - lang, 1), 0) + lang >= text_at
    gv = jnp.where(rows_v, gf[0:vis].astype(F32), 0.0)
    gl = jnp.where(rows_l, gf[lang:].astype(F32), 0.0)
    pre_v = (dot(gv.astype(BF), wov[0], NT) * slv[...].astype(F32)).astype(BF)
    pre_l = (dot(gl.astype(BF), wol[0], NT) * sll[...].astype(F32)).astype(BF)
    hsum[0:1] = jnp.sum(pre_v.astype(F32), axis=0, keepdims=True)
    hsum[1:2] = jnp.sum(pre_l.astype(F32), axis=0, keepdims=True)
    part_v = dot(pre_v, wv[0], NT)
    part_l = dot(pre_l, wl[0], NT)

    @pl.when(t == 0)
    def _():
        acc[...] = jnp.zeros_like(acc)

    acc[0:vis] += part_v
    acc[lang:] += part_l

    @pl.when(t == pl.num_programs(0) - 1)
    def _():
        sums[3:4] = jnp.sum(gv, axis=0, keepdims=True)
        sums[4:5] = jnp.sum(gl, axis=0, keepdims=True)
        finish_ff_back(dm, g, acc[...], x1, gain, go, ga, sums)


def back_ff_two(dm, layer, g, gf, x1, norm_gain, slope_v, slope_l, ffn_in, ffn_out):
    d, live, hid = dm.width, dm.live, dm.hidden
    sds = jax.ShapeDtypeStruct
    return pl.pallas_call(
        functools.partial(back_ff_two_body, dm),
        grid=(hid // TILE,),
        in_specs=[
            whole((live, d)),
            whole((live, d)),
            whole((dm.full, d)),
            layer_block((2, d), layer),
            pl.BlockSpec((dm.vis, TILE), lambda t: (0, t)),
            pl.BlockSpec((live - dm.lang, TILE), lambda t: (0, t)),
            pl.BlockSpec((1, TILE, d), lambda t: (0, t, 0)),
            pl.BlockSpec((1, TILE, d), lambda t: (1, t, 0)),
            pl.BlockSpec((1, d, TILE), lambda t: (0, 0, t)),
            pl.BlockSpec((1, d, TILE), lambda t: (1, 0, t)),
        ],
        out_specs=[
            whole((live, d)),
            whole((live, d)),
            whole((5, d)),
            pl.BlockSpec((2, TILE), lambda t: (0, t)),
        ],
        out_shape=[sds((live, d), F32), sds((live, d), BF), sds((5, d), F32), sds((2, hid), F32)],
        scratch_shapes=[pltpu.VMEM((live, d), F32)],
        compiler_params=params(40),
        cost_estimate=cost(4 * live * d * hid, 22e6),
    )(g, gf, x1, norm_gain, slope_v, slope_l, ffn_out, ffn_out, ffn_in, ffn_in)


def back_attn_body(dm, g, ga, q, k, v, p, x, gain, win, wout, dqkv, go, gfo, sums):
    width, live = dm.width, dm.live
    gc = dot(ga[...], wout[0], NT).astype(BF)
    low_lane = lax.broadcasted_iota(jnp.int32, (1, 128), 1) < 64
    for pair in range(HEADS // 2):
        lanes = slice(pair * 128, pair * 128 + 128)
        gp, qp, kp, vp = gc[:, lanes], q[:, lanes], k[:, lanes], v[:, lanes]
        dqs, dks, dvs = [], [], []
        for j in range(2):
            gm = jnp.where(low_lane if j == 0 else ~low_lane, gp, jnp.zeros_like(gp))
            dprob = dot(gm, vp, NT)
            prob_low = p[2 * pair + j]
            prob = prob_low.astype(F32)
            inner = jnp.sum(prob * dprob, axis=-1, keepdims=True)
            ds = (prob * (dprob - inner)).astype(BF)
            dqs.append(dot(ds, kp))
            dks.append(dot(ds, qp, TN))
            dvs.append(dot(prob_low, gp, TN))
        dq = jnp.where(low_lane, dqs[0], dqs[1]) * 0.125
        dk = jnp.where(low_lane, dks[0], dks[1])
        dv = jnp.where(low_lane, dvs[0], dvs[1])
        dqkv[:, pair * 128 : pair * 128 + 128] = dq.astype(BF)
        dqkv[:, width + pair * 128 : width + pair * 128 + 128] = dk[:live].astype(BF)
        dqkv[:, 2 * width + pair * 128 : 2 * width + pair * 128 + 128] = dv[:live].astype(BF)
    packed = dqkv[...]
    gn = dot(packed, win[0], NT)
    grad_in, gain_sum, offset_sum = norm_back(gn, x[0:live].astype(F32), gain[0, 0:1].astype(F32))
    out = g[...] + grad_in
    go[...] = out
    gfo[...] = out.astype(BF)
    sums[0:1] = gain_sum
    sums[1:2] = offset_sum
    sums[2:3] = jnp.sum(packed[:, 0:width].astype(F32), axis=0, keepdims=True)
    sums[3:4] = jnp.sum(packed[:, 2 * width :].astype(F32), axis=0, keepdims=True)


def back_attn(dm, layer, g, ga, q, k, v, p, x, norm_gain, attn_in, attn_out):
    d, live, keys = dm.width, dm.live, dm.keys
    sds = jax.ShapeDtypeStruct
    shapes = [sds((live, 3 * d), BF), sds((live, d), F32), sds((live, d), BF), sds((4, d), F32)]
    return pl.pallas_call(
        functools.partial(back_attn_body, dm),
        grid=(1,),
        in_specs=[
            whole((live, d)),
            whole((live, d)),
            whole((live, d)),
            whole((keys, d)),
            whole((keys, d)),
            whole((HEADS, live, keys)),
            whole((dm.full, d)),
            layer_block((2, d), layer),
            layer_block((d, 3 * d), layer),
            layer_block((d, d), layer),
        ],
        out_specs=[whole(s.shape) for s in shapes],
        out_shape=shapes,
        compiler_params=params(40),
        cost_estimate=cost(2 * live * d * d * 4 + 10 * live * keys * d, 10e6),
    )(g, ga, q, k, v, p, x, norm_gain, attn_in, attn_out)


def store_shares(dm, ref, lead, row, value, flip):
    n, share = dm.item_devs, dm.share
    bits = n.bit_length() - 1
    for i in range(n):
        place = int(format(i, "0%db" % bits)[::-1], 2) if bits else 0
        ref[lead + (place ^ flip, slice(row, row + share))] = value[i * share : (i + 1) * share]


def in_kernel_shares(dm):
    return dm.share % 16 == 0


def wgrad_attn_body(dm, sc, n1, dqkv, ctx, ga, out):
    width = dm.width
    for quarter in range(4):
        if quarter < 3:
            value = dot(n1[...], dqkv[:, quarter * width : (quarter + 1) * width], TN).astype(BF)
        else:
            value = dot(ctx[...], ga[...], TN).astype(BF)
        if in_kernel_shares(dm):
            store_shares(dm, out, (quarter ^ sc[1],), 0, value, sc[2])
        else:
            out[quarter ^ sc[1]] = value


def wgrad_attn(dm, sc, n1, dqkv, ctx, ga):
    d, live, n, share = dm.width, dm.live, dm.item_devs, dm.share
    shape = (4, n, share, d) if in_kernel_shares(dm) else (4, d, d)
    out = pl.pallas_call(
        functools.partial(wgrad_attn_body, dm),
        grid=(1,),
        in_specs=[SMEM, whole((live, d)), whole((live, 3 * d)), whole((live, d)), whole((live, d))],
        out_specs=whole(shape),
        out_shape=jax.ShapeDtypeStruct(shape, BF),
        compiler_params=params(40),
        cost_estimate=cost(8 * live * d * d, 8e6),
    )(sc, n1, dqkv, ctx, ga)
    return out


def wgrad_ff_body(dm, experts, sc, *refs):
    d, live, streams = dm.width, dm.live, dm.streams
    n2s = refs[0:streams]
    gfs = refs[streams : 2 * streams]
    wi, wo, bi, out, n2a, gfa, acta, gpa = refs[2 * streams :]
    base = 0
    for index, (expert, start, stop, low, high) in enumerate(experts):
        size = stop - start
        total = size * streams
        rows = lax.broadcasted_iota(jnp.int32, (size, 1), 0) + start
        keep = (rows >= low) & (rows < high)
        for r in range(streams):
            n2a[r * size : (r + 1) * size] = n2s[r][start:stop]
            gpart = gfs[r][start:stop]
            if low > start or high < stop:
                gpart = jnp.where(keep, gpart.astype(F32), 0.0).astype(BF)
            gfa[r * size : (r + 1) * size] = gpart

        chunk = size if size >= 128 else total

        def step(c, carry, index=index, chunk=chunk):
            at = pl.ds(pl.multiple_of(c * chunk, 16), chunk)
            act, slope = gelu_parts(dot(n2a[at], wi[index]) + bi[index].astype(F32))
            acta[at] = act.astype(BF)
            gpa[at] = (dot(gfa[at], wo[index], NT) * slope).astype(BF)
            return carry

        lax.fori_loop(0, total // chunk, step, 0)
        grads = (
            (n2a, gpa),
            (acta, gfa),
        )
        for left, right in grads:
            value = dot(left[0:total], right[0:total], TN).astype(BF)
            if in_kernel_shares(dm):
                store_shares(dm, out, (), base, value, sc[2])
                base += dm.share
            else:
                out[base] = value
                base += 1


def wgrad_ff(dm, experts, sc, n2s, gfs, wi, wo, bi):
    d, live, n, share = dm.width, dm.live, dm.item_devs, dm.share
    count = len(experts)
    shape = (n, 2 * count * share, d) if in_kernel_shares(dm) else (2 * count, d, d)
    top = max(stop - start for _, start, stop, _, _ in experts) * dm.streams
    return pl.pallas_call(
        functools.partial(wgrad_ff_body, dm, experts),
        grid=(1,),
        in_specs=[SMEM] + [whole((live, d))] * (2 * dm.streams) + [whole((count, d, d)), whole((count, d, d)), whole((count, 1, d))],
        out_specs=whole(shape),
        out_shape=jax.ShapeDtypeStruct(shape, BF),
        scratch_shapes=[pltpu.VMEM((top, d), BF)] * 4,
        compiler_params=params(48),
        cost_estimate=cost(8 * live * 4 * d * d, 12e6, 2 * live * 4 * d),
    )(sc, *n2s, *gfs, wi, wo, bi)


def swap(value, axis, bit):
    size = lax.axis_size(axis)
    return lax.ppermute(value, axis, [(i, i ^ bit) for i in range(size)])


def by_index(blocks, index):
    return lax.dynamic_index_in_dim(blocks, index, 0, keepdims=False)


def exchange(blocks, stream):
    rel = [by_index(blocks, stream ^ r) for r in range(4)]
    far = swap(jnp.stack([rel[2], rel[3]]), "stream", 2)
    near = swap(jnp.stack([rel[1], far[1]]), "stream", 1)
    got = jnp.stack([rel[0], near[0], far[0], near[1]])
    return jnp.stack([by_index(got, stream ^ r) for r in range(4)])


def gather_rel(value):
    far = swap(value, "stream", 2)
    near = swap(value, "stream", 1)
    both = swap(far, "stream", 1)
    return [value, near, far, both]


def halve_items(value):
    bit = 1
    while bit < lax.axis_size("items"):
        half = value.shape[0] // 2
        value = value[:half] + swap(value[half:], "items", bit)
        bit *= 2
    return value[0]


def gather_quarters(value, stream):
    far = swap(value, "stream", 2)
    pair = jnp.stack([value, far])
    near = swap(pair, "stream", 1)
    got = jnp.stack([pair[0], near[0], pair[1], near[1]])
    return [by_index(got, stream ^ r) for r in range(4)]


def reverse_bits(index, count):
    bits = count.bit_length() - 1
    out = index * 0
    for b in range(bits):
        out = out | (((index >> b) & 1) << (bits - 1 - b))
    return out


def per_device(
    tokens,
    cotangent,
    text_len,
    attn_in,
    attn_bias,
    attn_out,
    out_bias,
    norm_gain,
    norm_bias,
    ffn_in,
    ffn_in_bias,
    ffn_out,
    ffn_out_bias,
):
    streams = lax.axis_size("stream")
    item_devs = lax.axis_size("items")
    stream = lax.axis_index("stream")
    item = lax.axis_index("items")
    _, slots, width = tokens.shape
    hidden = ffn_in.shape[2]
    dm = Dims(slots, streams, width, hidden, item_devs)
    share = dm.share
    flip = reverse_bits(item, item_devs)
    own_len = by_index(text_len, stream)
    sc = jnp.stack([own_len, stream, flip]).astype(jnp.int32)

    x0 = exchange(tokens, stream).reshape(dm.rows, width)
    x0 = jnp.pad(x0, ((0, dm.full - dm.rows), (0, 0)))

    part = hidden // (item_devs * streams)
    wi_q = by_index(
        jnp.moveaxis(ffn_in.reshape(3, width, item_devs, streams, part), 3, 0), stream
    ).reshape(3, width, width)
    wo_q = by_index(
        jnp.moveaxis(ffn_out.reshape(3, item_devs, streams, part, width), 2, 0), stream
    ).reshape(3, width, width)
    bi_q = by_index(
        jnp.moveaxis(ffn_in_bias.reshape(3, item_devs, streams, part), 2, 0), stream
    ).reshape(3, 1, width)

    a0 = fwd_attn(dm, 0, sc, x0, norm_gain, norm_bias, attn_in, attn_bias, attn_out, out_bias)
    n1_0, q_0, k_0, v_0, p_0, ctx_0, x1_0, n2_0, n2l_0 = a0
    n2_all_0 = gather_rel(n2l_0)
    sv_0, sl_0, x2_0 = fwd_ff_two(dm, n2_0, x1_0, ffn_in, ffn_in_bias, ffn_out, ffn_out_bias)
    a1 = fwd_attn(dm, 1, sc, x2_0, norm_gain, norm_bias, attn_in, attn_bias, attn_out, out_bias)
    n1_1, q_1, k_1, v_1, p_1, ctx_1, x1_1, n2_1, n2l_1 = a1
    n2_all_1 = gather_rel(n2l_1)
    s_1, mixed_own = fwd_ff_one(dm, 2, n2_1, x1_1, ffn_in, ffn_in_bias, ffn_out, ffn_out_bias)
    mixed = exchange(mixed_own[: dm.rows].reshape(streams, slots, width), stream)

    cot = exchange(cotangent, stream).reshape(dm.rows, width)[: dm.live]
    row = jnp.arange(dm.live, dtype=jnp.int32)
    live_row = (row < PATCHES) | ((row >= dm.text_at) & (row < dm.text_at + own_len))
    gf_1 = jnp.where(live_row[:, None], cot, jnp.zeros_like(cot))
    gf_all_1 = gather_rel(gf_1)
    g, ga_1, fs_1, hs_1 = back_ff_one(dm, 1, 2, gf_1.astype(F32), gf_1, x1_1, norm_gain, s_1, ffn_in, ffn_out)
    live, vis, lang, text_at = dm.live, dm.vis, dm.lang, dm.text_at
    join = wgrad_ff(dm, ((2, 0, live, 0, live),), sc, n2_all_1, gf_all_1, wi_q[2:3], wo_q[2:3], bi_q[2:3])
    dqkv_1, g, gf_0, as_1 = back_attn(dm, 1, g, ga_1, q_1, k_1, v_1, p_1, x2_0, norm_gain, attn_in, attn_out)
    att_1 = wgrad_attn(dm, sc, n1_1, dqkv_1, ctx_1, ga_1)
    gf_all_0 = gather_rel(gf_0)
    g, ga_0, fs_0, hs_0 = back_ff_two(dm, 0, g, gf_0, x1_0, norm_gain, sv_0, sl_0, ffn_in, ffn_out)
    two = wgrad_ff(
        dm,
        ((0, 0, vis, 0, text_at), (1, lang, live, text_at, live)),
        sc, n2_all_0, gf_all_0, wi_q[0:2], wo_q[0:2], bi_q[0:2],
    )
    dqkv_0, g, _, as_0 = back_attn(dm, 0, g, ga_0, q_0, k_0, v_0, p_0, x0, norm_gain, attn_in, attn_out)
    att_0 = wgrad_attn(dm, sc, n1_0, dqkv_0, ctx_0, ga_0)

    if not in_kernel_shares(dm):
        order = jnp.stack([reverse_bits(jnp.int32(i), item_devs) for i in range(item_devs)]) ^ item

        def reorder(value, lead):
            value = value.reshape(value.shape[:lead] + (item_devs, share, width))
            return jnp.take(value, order, axis=lead)

        join = jnp.moveaxis(reorder(join, 1), 0, 1).reshape(item_devs, 2 * share, width)
        two = jnp.moveaxis(reorder(two, 1), 0, 1).reshape(item_devs, 4 * share, width)
        att_1 = reorder(att_1, 1)
        att_0 = reorder(att_0, 1)

    def halve_stream(value):
        near = swap(jnp.stack([value[1], value[3]]), "stream", 1)
        low = value[0] + near[0]
        high = value[2] + near[1]
        return low + swap(high, "stream", 2)

    join_q = gather_quarters(halve_items(join), stream)
    att_1_q = gather_quarters(halve_items(halve_stream(att_1)), stream)
    two_q = gather_quarters(halve_items(two), stream)
    att_0_q = gather_quarters(halve_items(halve_stream(att_0)), stream)

    def ffn_outs(quarters, base):
        ins = jnp.stack([value[base : base + share] for value in quarters])
        outs = jnp.concatenate([value[base + share : base + 2 * share] for value in quarters], axis=0)
        ins = ins.reshape(streams, share, item_devs, part)
        ins = jnp.transpose(ins, (1, 2, 0, 3)).reshape(share, hidden)
        return ins.astype(F32), outs.astype(F32)

    join_in, join_out = ffn_outs(join_q, 0)
    vis_in, vis_out = ffn_outs(two_q, 0)
    lan_in, lan_out = ffn_outs(two_q, 2 * share)
    attn_in_grad = jnp.stack(
        [jnp.concatenate(att_0_q[:3], axis=-1), jnp.concatenate(att_1_q[:3], axis=-1)]
    ).astype(F32)
    attn_out_grad = jnp.stack([att_0_q[3], att_1_q[3]]).astype(F32)

    def shares(value):
        value = value.reshape(-1, item_devs, value.shape[-1] // item_devs)
        return jnp.moveaxis(value, 1, 0).reshape(item_devs, -1)

    pieces = [
        jnp.stack([as_0[2:4], as_1[2:4]]),
        jnp.stack([fs_0[2], fs_1[2]]),
        jnp.stack([jnp.stack([as_0[0], fs_0[0]]), jnp.stack([as_1[0], fs_1[0]])]),
        jnp.stack([jnp.stack([as_0[1], fs_0[1]]), jnp.stack([as_1[1], fs_1[1]])]),
        jnp.concatenate([hs_0, hs_1], axis=0),
        jnp.concatenate([fs_0[3:5], fs_1[3:4]], axis=0),
    ]
    flat = [shares(value) for value in pieces]
    small = jnp.concatenate(flat, axis=1)
    order = jnp.stack([reverse_bits(jnp.int32(i), item_devs) for i in range(item_devs)]) ^ item
    small = halve_items(jnp.take(small, order, axis=0))
    small = small + swap(small, "stream", 1)
    small = small + swap(small, "stream", 2)
    outs = []
    at = 0
    for value, columns in zip(pieces, flat):
        size = columns.shape[1]
        outs.append(small[at : at + size].reshape(value.shape[:-1] + (value.shape[-1] // item_devs,)))
        at += size

    g = jnp.pad(g.astype(BF), ((0, dm.rows - dm.live), (0, 0)))
    tokens_grad = exchange(g.reshape(streams, slots, width), stream).astype(F32)
    return (
        mixed,
        tokens_grad,
        attn_in_grad,
        outs[0],
        attn_out_grad,
        outs[1],
        outs[2],
        outs[3],
        jnp.stack([vis_in, lan_in, join_in]),
        outs[4],
        jnp.stack([vis_out, lan_out, join_out]),
        outs[5],
    )


def solution(mesh):
    return jax.shard_map(
        per_device,
        mesh=mesh,
        in_specs=(
            P("items", "stream", None),
            P("items", "stream", None),
            P("items"),
            P(),
            P(),
            P(),
            P(),
            P(),
            P(),
            P(),
            P(),
            P(),
            P(),
        ),
        out_specs=(
            P("items", "stream", None),
            P("items", "stream", None),
            P(None, "items", None),
            P(None, None, "items"),
            P(None, "items", None),
            P(None, "items"),
            P(None, None, "items"),
            P(None, None, "items"),
            P(None, "items", None),
            P(None, "items"),
            P(None, "items", None),
            P(None, "items"),
        ),
        check_vma=False,
    )
```

time: 2630 us -> 405 us (0.15)
  waiting for transfers between devices: 2170 us -> 153 us
  matrix products: 146 us -> 0 us
  Pallas kernels: 0 us -> 88.4 us
  blocking collectives: 69.5 us -> 0 us
  other arithmetic: 76.7 us -> 27.3 us
  local copies, waits for them, and re-layouts: 136 us -> 90.9 us
  starting transfers between devices: 1.76 us -> 36.1 us
    reduce_scatter x10 -> x0, waiting for transfers between devices: 1260 us -> none  [the longest x2 470 us: per_device(): lax.psum_scatter(ffn_pieces[0], 'items', scatter_dimension=1, tiled=True)]
    unnamed x50 -> x0, waiting for transfers between devices: 827 us -> none
    ppermute x0 -> x49, waiting for transfers between devices: none -> 153 us  [swap(): return lax.ppermute(value, axis, [(i, i ^ bit) for i in range(size)])]
    dot_general x34 -> x0, matrix products: 135 us -> none  [the longest x8 34.9 us: weight_grad(): jnp.einsum('isd,isf->df', left, right, preferred_element_type=jnp.float32)]
    pallas_call x0 -> x12, Pallas kernels: none -> 88.4 us  [the longest x2 20.5 us: wgrad_ff(): pl.pallas_call(functools.partial(wgrad_ff_body, dm, experts), grid=(1,),...]
    all_gather x6 -> x0, waiting for transfers between devices: 78.6 us -> none  [the longest x2 32.7 us: per_device(): lax.all_gather(keys_own, 'stream', axis=1, tiled=True)]
    all_gather x6 -> x0, blocking collectives: 39.6 us -> none  [the longest x2 13.2 us: per_device(): lax.all_gather(quarters[0].astype(jnp.bfloat16), 'stream', axis=1, tiled=...]
    ppermute x0 -> x49, starting transfers between devices: none -> 36.1 us  [swap(): return lax.ppermute(value, axis, [(i, i ^ bit) for i in range(size)])]
  transfers between devices with their start and end apart: 33 -> 49, of which waited for: 33 -> 21; matrix products, arithmetic and copies ran while one was open for 9% -> 22% of each run, Pallas kernels for 0% -> 22%
where the time goes in v1:
time: 405 us; the launch traced here: 399 us
  waiting for transfers between devices  153 us (38%)
  local copies, waits for them, and re-layouts  90.9 us (22%)
  Pallas kernels  88.4 us (22%)
  starting transfers between devices  36.1 us (9%)
  other arithmetic  27.3 us (7%)
    ppermute x49, waiting for transfers between devices, swap(): return lax.ppermute(value, axis, [(i, i ^ bit) for i in range(size)])  153 us
    ppermute x49, starting transfers between devices, swap(): return lax.ppermute(value, axis, [(i, i ^ bit) for i in range(size)])  36.1 us
    unnamed x126, local copies, waits for them, and re-layouts  32 us
    pallas_call x2, Pallas kernels, wgrad_ff(): pl.pallas_call(functools.partial(wgrad_ff_body, dm, experts), grid=(1,),...  20.5 us
    pallas_call x2, Pallas kernels, back_attn(): pl.pallas_call(functools.partial(back_attn_body, dm), grid=(1,), in_specs...  17.4 us
    dynamic_slice x11, local copies, waits for them, and re-layouts, by_index(): return lax.dynamic_index_in_dim(blocks, index, 0, keepdims=False)  14.2 us
    pallas_call x2, Pallas kernels, fwd_attn(): pl.pallas_call(functools.partial(fwd_attn_body, dm), grid=(1,), in_specs=...  13 us
    pallas_call x1, Pallas kernels, back_ff_two(): pl.pallas_call(functools.partial(back_ff_two_body, dm), grid=(hid // TILE...  10.8 us
  transfers between devices with their start and end apart: 49, of which 21 were waited for; matrix products, arithmetic and copies ran while one was open for 22% of the time, Pallas kernels for 22%

profile of v1, /device:TPU:0, one launch (start us, length us, event | category | flops | bytes accessed | tf_op | source)
XLA Modules:
  0.0 399.4 jit_solution(15861203038689882259)
XLA Ops:
  0.7 3.0 constant_dynamic-slice_fusion.59
  4.9 2.9 collective-permute-start
  12.7 3.1 dynamic-slice_bitcast_fusion.1
  18.5 18.5 %copy.59 = bf16[3,768,3072]{1,2,0:T(8,128)(2,1)} copy(bf16[3,768,3072]{2,1,0:T(8,128)(2,1)} %wl.3) | data formatting | bytes 28311552 | tf_op args[9]
  37.0 2.2 dynamic-slice_bitcast_fusion
  39.2 2.4 constant_dynamic-slice_fusion.5
  41.8 2.5 copy.62.refs_8_
  44.3 2.6 copy.66.refs_8_
  54.3 2.1 collective-permute-start.42
  61.4 1.9 reshape.440
  64.4 6.4 %shard_map.220 = (bf16[240,768]{1,0:T(8,128)(2,1)S(1)}, bf16[240,768]{1,0:T(8,128)(2,1)S(1)}, bf16[256,768]{1,0:T(8,128)(2,1)S(1)}, bf16[256,768]{1,0:T(8,128)(2...) custom-call(s32[3]{0:T(128)S(1)} %pad_add_fusion.sc, ...), custom_call_target="tpu_custom_call" | custom-call | flops 1497366528 | bytes 8000000 | tf_op jit(solution)/shard_map/pallas_call | solution.py:142
  73.0 8.9 %shard_map.221 = (bf16[208,3072]{1,0:T(8,128)(2,1)S(1)}, bf16[48,3072]{1,0:T(8,128)(2,1)S(1)}, f32[272,768]{1,0:T(8,128)S(1)}) custom-call(bf16[272,768]{1,0:T(8,128)(2,1)S(1)} %get-tuple-element.50.n2, f32[272,768]{1,0:T(8,128)S(1)} %get-tuple-element.51.x1, bf16[3,768,3072]{2,1,0:T(8,128)(2,1)} %wl.3, bf16[3,768,3072]{2,1,0:T(8,128)(2,1)} %wl.3, ...), custom_call_target="tpu_custom_call" | custom-call | flops 2566914048 | bytes 21000000 | tf_op jit(solution)/shard_map/pallas_call | solution.py:241
  81.9 6.6 %shard_map.222 = (bf16[240,768]{1,0:T(8,128)(2,1)S(1)}, bf16[240,768]{1,0:T(8,128)(2,1)S(1)}, bf16[256,768]{1,0:T(8,128)(2,1)S(1)}, bf16[256,768]{1,0:T(8,128)(2...) custom-call(s32[3]{0:T(128)S(1)} %pad_add_fusion.sc, ...), custom_call_target="tpu_custom_call" | custom-call | flops 1497366528 | bytes 8000000 | tf_op jit(solution)/shard_map/pallas_call | solution.py:142
  89.8 6.7 %shard_map.223 = (bf16[240,3072]{1,0:T(8,128)(2,1)S(1)}, bf16[272,768]{1,0:T(8,128)(2,1)S(1)}) custom-call(bf16[272,768]{1,0:T(8,128)(2,1)S(1)} %get-tuple-element.53.n2, f32[272,768]{1,0:T(8,128)S(1)} %get-tuple-element.54.x1, bf16[3,768,3072]{2,1,0:T(8,128)(2,1)} %wl.3, bf16[3,1,3072]{2,1,0:T(2,128)(2,1)S(1)} %copy.48.bi, bf16[3,3072,768]{2,1,0:T(8,128)(2,1)} %wol.3, ...), custom_call_target="tpu_custom_call" | custom-call | flops 2566914048 | bytes 12000000 | tf_op jit(solution)/shard_map/pallas_call | solution.py:188
  96.5 7.0 %shard_map.224 = (f32[240,768]{1,0:T(8,128)S(1)}, bf16[240,768]{1,0:T(8,128)(2,1)S(1)}, f32[4,768]{1,0:T(4,128)S(1)}, f32[1,3072]{1,0:T(1,128)S(1)}) custom-call(f32[240,768]{1,0:T(8,128)S(1)} %get-tuple-element.100.g, bf16[240,768]{1,0:T(8,128)(2,1)S(1)} %get-tuple-element.101.gf.refs_4_, f32[272,768]{1,0:T(8,128)S(1)} %get-tuple-element.54.x1, ...), custom_call_target="tpu_custom_call" | custom-call | flops 2264924160 | bytes 13000000 | tf_op jit(solution)/shard_map/pallas_call | solution.py:300
  103.6 8.4 %shard_map.225 = (bf16[240,2304]{1,0:T(8,128)(2,1)S(1)}, f32[240,768]{1,0:T(8,128)S(1)}, bf16[240,768]{1,0:T(8,128)(2,1)S(1)}, f32[4,768]{1,0:T(4,128)S(1)}) custom-call(f32[240,768]{1,0:T(8,128)S(1)} %get-tuple-element.57.g, bf16[240,768]{1,0:T(8,128)(2,1)S(1)} %get-tuple-element.58.ga, bf16[240,768]{1,0:T(8,128)(2,1)S(1)} %get-tuple-element.59.q, ...), custom_call_target="tpu_custom_call" | custom-call | flops 1604321280 | bytes 10000000 | tf_op jit(solution)/shard_map/pallas_call | solution.py:424
  112.9 10.8 %shard_map.226 = (f32[240,768]{1,0:T(8,128)S(1)}, bf16[240,768]{1,0:T(8,128)(2,1)S(1)}, f32[5,768]{1,0:T(8,128)S(1)}, f32[2,3072]{1,0:T(2,128)S(1)}) custom-call(f32[240,768]{1,0:T(8,128)S(1)} %get-tuple-element.63.g, bf16[240,768]{1,0:T(8,128)(2,1)S(1)} %get-tuple-element.64.gf.refs_4_, f32[272,768]{1,0:T(8,128)S(1)} %get-tuple-element.51.x1, ...), custom_call_target="tpu_custom_call" | custom-call | flops 2264924160 | bytes 22000000 | tf_op jit(solution)/shard_map/pallas_call | solution.py:356
  123.8 9.0 %shard_map.227 = (bf16[240,2304]{1,0:T(8,128)(2,1)S(1)}, f32[240,768]{1,0:T(8,128)S(1)}, bf16[240,768]{1,0:T(8,128)(2,1)}, f32[4,768]{1,0:T(4,128)S(1)}) custom-call(f32[240,768]{1,0:T(8,128)S(1)} %get-tuple-element.67.g, bf16[240,768]{1,0:T(8,128)(2,1)S(1)} %get-tuple-element.68.ga, bf16[240,768]{1,0:T(8,128)(2,1)S(1)} %get-tuple-element.69.q, ...), custom_call_target="tpu_custom_call" | custom-call | flops 1604321280 | bytes 10000000 | tf_op jit(solution)/shard_map/pallas_call | solution.py:424
  136.7 1.9 collective-permute-start.22
  138.6 2.0 shard_map.228
  140.8 2.2 copy-done.2
  143.8 2.0 shard_map.229
  146.0 2.0 copy-done.1
  154.7 2.0 reshape.441
  157.5 2.7 collective-permute-start.24
  160.2 1.8 constant_dynamic-slice_fusion.51
  165.0 1.7 pad_maximum_fusion.19
  176.9 4.0 collective-permute-done.2
  183.6 9.1 %shard_map.231 = bf16[8,192,768]{2,1,0:T(8,128)(2,1)} custom-call(s32[3]{0:T(128)S(1)} %pad_add_fusion.sc, bf16[240,768]{1,0:T(8,128)(2,1)} %get-tuple-element.87.refs_0_, bf16[240,768]{1,0:T(8,128)(2,1)} %collective-permute-done.38.refs_1_, bf16[240,768]{1,0:T(8,128)(2,1)} %collective-permute-done.39.refs_2_, ...), custom_call_target="tpu_custom_call" | custom-call | flops 4529848320 | bytes 12000000 | tf_op jit(solution)/shard_map/pallas_call | solution.py:533
  192.7 2.5 slice.614
  195.4 2.2 collective-permute-done.31.refs_6_
  200.4 11.3 %shard_map.230 = bf16[8,384,768]{2,1,0:T(8,128)(2,1)} custom-call(s32[3]{0:T(128)S(1)} %pad_add_fusion.sc, bf16[240,768]{1,0:T(8,128)(2,1)S(1)} %copy-done.31, bf16[240,768]{1,0:T(8,128)(2,1)S(1)} %collective-permute-done.27.refs_1_, bf16[240,768]{1,0:T(8,128)(2,1)S(1)} %collective-permute-done.28.refs_2_, ...), custom_call_target="tpu_custom_call" | custom-call | flops 4529848320 | bytes 12000000 | tf_op jit(solution)/shard_map/pallas_call | solution.py:533
  211.7 2.0 slice.604
  216.3 10.2 %collective-permute-done.44 = bf16[4,192,768]{2,1,0:T(8,128)(2,1)S(1)} collective-permute-done((bf16[4,192,768]{2,1,0:T(8,128)(2,1)}, bf16[4,192,768]{2,1,0:T(8,128)(2,1)S(1)}, u32[]{:S(2)}, u32[]{:S(2)}) %collective-permute-start.44) | collective-permute-done | bytes 1179680 | tf_op jit(solution)/shard_map/ppermute | solution.py:547
  228.5 12.9 %collective-permute-done.45 = bf16[2,192,768]{2,1,0:T(8,128)(2,1)S(1)} collective-permute-done((bf16[2,192,768]{2,1,0:T(8,128)(2,1)S(1)}, bf16[2,192,768]{2,1,0:T(8,128)(2,1)S(1)}, u32[]{:S(2)}, u32[]{:S(2)}) %collective-permute-start.45) | collective-permute-done | bytes 589856 | tf_op jit(solution)/shard_map/ppermute | solution.py:547
  241.5 2.6 collective-permute-start.46
  246.0 10.1 %collective-permute-done.46 = bf16[1,192,768]{2,1,0:T(8,128)(2,1)S(1)} collective-permute-done((bf16[1,192,768]{2,1,0:T(8,128)(2,1)S(1)}, bf16[1,192,768]{2,1,0:T(8,128)(2,1)S(1)}, u32[]{:S(2)}, u32[]{:S(2)}) %collective-permute-start.46) | collective-permute-done | bytes 294944 | tf_op jit(solution)/shard_map/ppermute | solution.py:547
  256.4 20.3 %collective-permute-done.33 = bf16[4,384,768]{2,1,0:T(8,128)(2,1)S(1)} collective-permute-done((bf16[4,384,768]{2,1,0:T(8,128)(2,1)S(1)}, bf16[4,384,768]{2,1,0:T(8,128)(2,1)S(1)}, u32[]{:S(2)}, u32[]{:S(2)}) %collective-permute-start.33) | collective-permute-done | bytes 2359328 | tf_op jit(solution)/shard_map/ppermute | solution.py:547
  277.6 9.4 %collective-permute-done.47 = bf16[192,768]{1,0:T(8,128)(2,1)S(1)} collective-permute-done((bf16[192,768]{1,0:T(8,128)(2,1)S(1)}, bf16[192,768]{1,0:T(8,128)(2,1)S(1)}, u32[]{:S(2)}, u32[]{:S(2)}) %collective-permute-start.47) | collective-permute-done | bytes 294944 | tf_op jit(solution)/shard_map/ppermute | solution.py:547
  290.9 12.8 %collective-permute-done.10 = bf16[4,96,768]{2,1,0:T(8,128)(2,1)S(1)} collective-permute-done((bf16[4,96,768]{2,1,0:T(8,128)(2,1)S(1)}, bf16[4,96,768]{2,1,0:T(8,128)(2,1)S(1)}, u32[]{:S(2)}, u32[]{:S(2)}) %collective-permute-start.10) | collective-permute-done | bytes 589856 | tf_op jit(solution)/shard_map/ppermute | solution.py:547
  304.7 11.2 %collective-permute-done.17 = bf16[4,96,768]{2,1,0:T(8,128)(2,1)S(1)} collective-permute-done((bf16[4,96,768]{2,1,0:T(8,128)(2,1)S(1)}, bf16[4,96,768]{2,1,0:T(8,128)(2,1)S(1)}, u32[]{:S(2)}, u32[]{:S(2)}) %collective-permute-start.17) | collective-permute-done | bytes 589856 | tf_op jit(solution)/shard_map/ppermute | solution.py:547
  317.1 2.6 collective-permute-start.35
  320.2 11.0 %collective-permute-done.18 = bf16[2,96,768]{2,1,0:T(8,128)(2,1)S(1)} collective-permute-done((bf16[2,96,768]{2,1,0:T(8,128)(2,1)S(1)}, bf16[2,96,768]{2,1,0:T(8,128)(2,1)S(1)}, u32[]{:S(2)}, u32[]{:S(2)}) %collective-permute-start.18) | collective-permute-done | bytes 294944 | tf_op jit(solution)/shard_map/ppermute | solution.py:547
  331.4 25.1 %collective-permute-done.12 = bf16[1,96,768]{2,1,0:T(8,128)(2,1)S(1)} collective-permute-done((bf16[1,96,768]{2,1,0:T(8,128)(2,1)S(1)}, bf16[1,96,768]{2,1,0:T(8,128)(2,1)S(1)}, u32[]{:S(2)}, u32[]{:S(2)}) %collective-permute-start.12) | collective-permute-done | bytes 147488 | tf_op jit(solution)/shard_map/ppermute | solution.py:547
  358.8 3.6 collective-permute-done.13
  365.9 14.1 %collective-permute-done.36 = bf16[384,768]{1,0:T(8,128)(2,1)S(1)} collective-permute-done((bf16[384,768]{1,0:T(8,128)(2,1)S(1)}, bf16[384,768]{1,0:T(8,128)(2,1)S(1)}, u32[]{:S(2)}, u32[]{:S(2)}) %collective-permute-start.36) | collective-permute-done | bytes 589856 | tf_op jit(solution)/shard_map/ppermute | solution.py:547
  394.9 2.1 maximum_convert_fusion
  397.0 1.9 maximum_convert_fusion.1
  (380 shorter events, 91.7 us)
Async XLA Ops:
  4.9 44.1 %collective-permute-start = (bf16[2,66,768]{2,0,1:T(2,128)(2,1)}, bf16[2,66,768]{2,0,1:T(2,128)(2,1)S(1)}, u32[]{:S(2)}, u32[]{:S(2)}) collective-permute-start(bf16[2,66,768]{2,0,1:T(2,128)(2,1)} %pad_maximum_fusion.21), channel_id=1, source_target_pairs={{0,16},{8,24},{16,0},{24,8},{1,17},{9,25},{17,1},{25,9},{2,18},{10... | collective-permute-start | bytes 608264 | tf_op jit(solution)/shard_map/ppermute | solution.py:547
  9.8 38.3 %collective-permute-start.4 = (bf16[2,66,768]{2,0,1:T(2,128)(2,1)}, bf16[2,66,768]{2,0,1:T(2,128)(2,1)S(1)}, u32[]{:S(2)}, u32[]{:S(2)}) collective-permute-start(bf16[2,66,768]{2,0,1:T(2,128)(2,1)} %pad_maximum_fusion.23), channel_id=1, source_target_pairs={{0,16},{8,24},{16,0},{24,8},{1,17},{9,25},{17,1},{25,9},{2,18},{10... | collective-permute-start | bytes 608264 | tf_op jit(solution)/shard_map/ppermute | solution.py:547
  48.9 2.0 collective-permute-start.5
  50.4 6.0 %collective-permute-start.1 = (bf16[2,66,768]{2,0,1:T(2,128)(2,1)}, bf16[2,66,768]{2,0,1:T(2,128)(2,1)}, u32[]{:S(2)}, u32[]{:S(2)}) collective-permute-start(bf16[2,66,768]{2,0,1:T(2,128)(2,1)} %pad_maximum_fusion.22), channel_id=1, source_target_pairs={{0,8},{8,0},{16,24},{24,16},{1,9},{9,1},{17,25},{25,17},{2,10},{10... | collective-permute-start | bytes 608264 | tf_op jit(solution)/shard_map/ppermute | solution.py:547
  54.3 116.4 %collective-permute-start.42 = (bf16[240,768]{1,0:T(8,128)(2,1)S(1)}, bf16[240,768]{1,0:T(8,128)(2,1)}, u32[]{:S(2)}, u32[]{:S(2)}) collective-permute-start(bf16[240,768]{1,0:T(8,128)(2,1)S(1)} %get-tuple-element.101.gf.refs_4_), channel_id=1, source_target_pairs={{0,16},{8,24},{16,0},{24,8},{1,17},{9,25},{17,1},{25,9},{2,18},{10... | collective-permute-start | bytes 1105928 | tf_op jit(solution)/shard_map/ppermute | solution.py:547
  56.4 125.1 %collective-permute-start.41 = (bf16[240,768]{1,0:T(8,128)(2,1)S(1)}, bf16[240,768]{1,0:T(8,128)(2,1)}, u32[]{:S(2)}, u32[]{:S(2)}) collective-permute-start(bf16[240,768]{1,0:T(8,128)(2,1)S(1)} %get-tuple-element.101.gf.refs_4_), channel_id=1, source_target_pairs={{0,8},{8,0},{16,24},{24,16},{1,9},{9,1},{17,25},{25,17},{2,10},{10... | collective-permute-start | bytes 1105928 | tf_op jit(solution)/shard_map/ppermute | solution.py:547
  89.2 81.5 %collective-permute-start.39 = (bf16[240,768]{1,0:T(8,128)(2,1)}, bf16[240,768]{1,0:T(8,128)(2,1)}, u32[]{:S(2)}, u32[]{:S(2)}) collective-permute-start(bf16[240,768]{1,0:T(8,128)(2,1)} %get-tuple-element.87.refs_0_), channel_id=1, source_target_pairs={{0,16},{8,24},{16,0},{24,8},{1,17},{9,25},{17,1},{25,9},{2,18},{10... | collective-permute-start | bytes 1105928 | tf_op jit(solution)/shard_map/ppermute | solution.py:547
  89.3 92.1 %collective-permute-start.38 = (bf16[240,768]{1,0:T(8,128)(2,1)}, bf16[240,768]{1,0:T(8,128)(2,1)}, u32[]{:S(2)}, u32[]{:S(2)}) collective-permute-start(bf16[240,768]{1,0:T(8,128)(2,1)} %get-tuple-element.87.refs_0_), channel_id=1, source_target_pairs={{0,8},{8,0},{16,24},{24,16},{1,9},{9,1},{17,25},{25,17},{2,10},{10... | collective-permute-start | bytes 1105928 | tf_op jit(solution)/shard_map/ppermute | solution.py:547
  136.7 14.8 %collective-permute-start.22 = (f32[4,2784]{1,0:T(4,128)S(1)}, f32[4,2784]{1,0:T(4,128)S(1)}, u32[]{:S(2)}, u32[]{:S(2)}) collective-permute-start(f32[4,2784]{1,0:T(4,128)S(1)} %slice.591), channel_id=1, source_target_pairs={{0,1},{1,0},{2,3},{3,2},{4,5},{5,4},{6,7},{7,6},{8,9},{9,8},{10,11... | collective-permute-start | bytes 133640 | tf_op jit(solution)/shard_map/ppermute | solution.py:547
  151.5 5.2 %collective-permute-start.23 = (f32[2,2784]{1,0:T(2,128)S(1)}, f32[2,2784]{1,0:T(2,128)}, u32[]{:S(2)}, u32[]{:S(2)}) collective-permute-start(f32[2,2784]{1,0:T(2,128)S(1)} %slice.593), channel_id=1, source_target_pairs={{0,2},{1,3},{2,0},{3,1},{4,6},{5,7},{6,4},{7,5},{8,10},{9,11},{10,... | collective-permute-start | bytes 66824 | tf_op jit(solution)/shard_map/ppermute | solution.py:547
  157.5 4.7 %collective-permute-start.24 = (f32[1,2784]{1,0:T(1,128)S(1)}, f32[1,2784]{1,0:T(1,128)S(1)}, u32[]{:S(2)}, u32[]{:S(2)}) collective-permute-start(f32[1,2784]{1,0:T(1,128)S(1)} %slice.595), channel_id=1, source_target_pairs={{0,4},{1,5},{2,6},{3,7},{4,0},{5,1},{6,2},{7,3},{8,12},{9,13},{10,... | collective-permute-start | bytes 33416 | tf_op jit(solution)/shard_map/ppermute | solution.py:547
  163.5 3.7 collective-permute-start.26
  167.2 7.0 %collective-permute-start.6 = (bf16[2,66,768]{2,1,0:T(8,128)(2,1)}, bf16[2,66,768]{2,1,0:T(8,128)(2,1)}, u32[]{:S(2)}, u32[]{:S(2)}) collective-permute-start(bf16[2,66,768]{2,1,0:T(8,128)(2,1)} %pad_maximum_fusion.19), channel_id=1, source_target_pairs={{0,16},{8,24},{16,0},{24,8},{1,17},{9,25},{17,1},{25,9},{2,18},{10... | collective-permute-start | bytes 608264 | tf_op jit(solution)/shard_map/ppermute | solution.py:547
  170.7 12.3 %collective-permute-start.43 = (bf16[240,768]{1,0:T(8,128)(2,1)}, bf16[240,768]{1,0:T(8,128)(2,1)}, u32[]{:S(2)}, u32[]{:S(2)}) collective-permute-start(bf16[240,768]{1,0:T(8,128)(2,1)} %collective-permute-done.42.refs_6_), channel_id=1, source_target_pairs={{0,8},{8,0},{16,24},{24,16},{1,9},{9,1},{17,25},{25,17},{2,10},{10... | collective-permute-start | bytes 1105928 | tf_op jit(solution)/shard_map/ppermute | solution.py:547
  170.7 12.5 %collective-permute-start.40 = (bf16[240,768]{1,0:T(8,128)(2,1)}, bf16[240,768]{1,0:T(8,128)(2,1)}, u32[]{:S(2)}, u32[]{:S(2)}) collective-permute-start(bf16[240,768]{1,0:T(8,128)(2,1)} %collective-permute-done.39.refs_2_), channel_id=1, source_target_pairs={{0,8},{8,0},{16,24},{24,16},{1,9},{9,1},{17,25},{25,17},{2,10},{10... | collective-permute-start | bytes 1105928 | tf_op jit(solution)/shard_map/ppermute | solution.py:547
  174.2 6.8 %collective-permute-start.2 = (bf16[2,66,768]{2,1,0:T(8,128)(2,1)}, bf16[2,66,768]{2,1,0:T(8,128)(2,1)S(1)}, u32[]{:S(2)}, u32[]{:S(2)}) collective-permute-start(bf16[2,66,768]{2,1,0:T(8,128)(2,1)} %pad_maximum_fusion.17), channel_id=1, source_target_pairs={{0,16},{8,24},{16,0},{24,8},{1,17},{9,25},{17,1},{25,9},{2,18},{10... | collective-permute-start | bytes 608264 | tf_op jit(solution)/shard_map/ppermute | solution.py:547
  180.9 14.3 %collective-permute-start.28 = (bf16[240,768]{1,0:T(8,128)(2,1)S(1)}, bf16[240,768]{1,0:T(8,128)(2,1)S(1)}, u32[]{:S(2)}, u32[]{:S(2)}) collective-permute-start(bf16[240,768]{1,0:T(8,128)(2,1)S(1)} %copy-done.31), channel_id=1, source_target_pairs={{0,16},{8,24},{16,0},{24,8},{1,17},{9,25},{17,1},{25,9},{2,18},{10... | collective-permute-start | bytes 1105928 | tf_op jit(solution)/shard_map/ppermute | solution.py:547
  181.5 16.1 %collective-permute-start.27 = (bf16[240,768]{1,0:T(8,128)(2,1)S(1)}, bf16[240,768]{1,0:T(8,128)(2,1)S(1)}, u32[]{:S(2)}, u32[]{:S(2)}) collective-permute-start(bf16[240,768]{1,0:T(8,128)(2,1)S(1)} %copy-done.31), channel_id=1, source_target_pairs={{0,8},{8,0},{16,24},{24,16},{1,9},{9,1},{17,25},{25,17},{2,10},{10... | collective-permute-start | bytes 1105928 | tf_op jit(solution)/shard_map/ppermute | solution.py:547
  181.5 16.1 %collective-permute-start.31 = (bf16[240,768]{1,0:T(8,128)(2,1)S(1)}, bf16[240,768]{1,0:T(8,128)(2,1)S(1)}, u32[]{:S(2)}, u32[]{:S(2)}) collective-permute-start(bf16[240,768]{1,0:T(8,128)(2,1)S(1)} %copy-done.25), channel_id=1, source_target_pairs={{0,16},{8,24},{16,0},{24,8},{1,17},{9,25},{17,1},{25,9},{2,18},{10... | collective-permute-start | bytes 1105928 | tf_op jit(solution)/shard_map/ppermute | solution.py:547
  183.0 15.1 %collective-permute-start.30 = (bf16[240,768]{1,0:T(8,128)(2,1)S(1)}, bf16[240,768]{1,0:T(8,128)(2,1)S(1)}, u32[]{:S(2)}, u32[]{:S(2)}) collective-permute-start(bf16[240,768]{1,0:T(8,128)(2,1)S(1)} %copy-done.25), channel_id=1, source_target_pairs={{0,8},{8,0},{16,24},{24,16},{1,9},{9,1},{17,25},{25,17},{2,10},{10... | collective-permute-start | bytes 1105928 | tf_op jit(solution)/shard_map/ppermute | solution.py:547
  183.2 44.7 %collective-permute-start.8 = (bf16[2,8,96,768]{3,2,1,0:T(8,128)(2,1)}, bf16[2,8,96,768]{3,2,1,0:T(8,128)(2,1)S(1)}, u32[]{:S(2)}, u32[]{:S(2)}) collective-permute-start(bf16[2,8,96,768]{3,2,1,0:T(8,128)(2,1)} %pad_maximum_fusion), channel_id=1, source_target_pairs={{0,8},{8,0},{16,24},{24,16},{1,9},{9,1},{17,25},{25,17},{2,10},{10... | collective-permute-start | bytes 7077896 | tf_op jit(solution)/shard_map/ppermute | solution.py:547
  195.2 4.6 %collective-permute-start.29 = (bf16[240,768]{1,0:T(8,128)(2,1)S(1)}, bf16[240,768]{1,0:T(8,128)(2,1)S(1)}, u32[]{:S(2)}, u32[]{:S(2)}) collective-permute-start(bf16[240,768]{1,0:T(8,128)(2,1)S(1)} %collective-permute-done.28.refs_2_), channel_id=1, source_target_pairs={{0,8},{8,0},{16,24},{24,16},{1,9},{9,1},{17,25},{25,17},{2,10},{10... | collective-permute-start | bytes 1105928 | tf_op jit(solution)/shard_map/ppermute | solution.py:547
  197.6 2.6 collective-permute-start.32
  197.6 29.0 %collective-permute-start.44 = (bf16[4,192,768]{2,1,0:T(8,128)(2,1)}, bf16[4,192,768]{2,1,0:T(8,128)(2,1)S(1)}, u32[]{:S(2)}, u32[]{:S(2)}) collective-permute-start(bf16[4,192,768]{2,1,0:T(8,128)(2,1)} %slice.614), channel_id=1, source_target_pairs={{0,1},{1,0},{2,3},{3,2},{4,5},{5,4},{6,7},{7,6},{8,9},{9,8},{10,11... | collective-permute-start | bytes 3538952 | tf_op jit(solution)/shard_map/ppermute | solution.py:547
  198.2 46.0 %collective-permute-start.15 = (bf16[2,8,96,768]{3,2,1,0:T(8,128)(2,1)S(1)}, bf16[2,8,96,768]{3,2,1,0:T(8,128)(2,1)S(1)}, u32[]{:S(2)}, u32[]{:S(2)}) collective-permute-start(bf16[2,8,96,768]{3,2,1,0:T(8,128)(2,1)S(1)} %copy-done.33), channel_id=1, source_target_pairs={{0,8},{8,0},{16,24},{24,16},{1,9},{9,1},{17,25},{25,17},{2,10},{10... | collective-permute-start | bytes 7077896 | tf_op jit(solution)/shard_map/ppermute | solution.py:547
  199.9 13.8 %collective-permute-start.7 = (bf16[2,66,768]{2,1,0:T(8,128)(2,1)}, bf16[2,66,768]{2,1,0:T(8,128)(2,1)S(1)}, u32[]{:S(2)}, u32[]{:S(2)}) collective-permute-start(bf16[2,66,768]{2,1,0:T(8,128)(2,1)} %pad_maximum_fusion.20), channel_id=1, source_target_pairs={{0,8},{8,0},{16,24},{24,16},{1,9},{9,1},{17,25},{25,17},{2,10},{10... | collective-permute-start | bytes 608264 | tf_op jit(solution)/shard_map/ppermute | solution.py:547
  200.2 15.2 %collective-permute-start.3 = (bf16[2,66,768]{2,1,0:T(8,128)(2,1)}, bf16[2,66,768]{2,1,0:T(8,128)(2,1)}, u32[]{:S(2)}, u32[]{:S(2)}) collective-permute-start(bf16[2,66,768]{2,1,0:T(8,128)(2,1)} %pad_maximum_fusion.18), channel_id=1, source_target_pairs={{0,8},{8,0},{16,24},{24,16},{1,9},{9,1},{17,25},{25,17},{2,10},{10... | collective-permute-start | bytes 608264 | tf_op jit(solution)/shard_map/ppermute | solution.py:547
  213.7 63.0 %collective-permute-start.33 = (bf16[4,384,768]{2,1,0:T(8,128)(2,1)S(1)}, bf16[4,384,768]{2,1,0:T(8,128)(2,1)S(1)}, u32[]{:S(2)}, u32[]{:S(2)}) collective-permute-start(bf16[4,384,768]{2,1,0:T(8,128)(2,1)S(1)} %slice.604), channel_id=1, source_target_pairs={{0,1},{1,0},{2,3},{3,2},{4,5},{5,4},{6,7},{7,6},{8,9},{9,8},{10,11... | collective-permute-start | bytes 7077896 | tf_op jit(solution)/shard_map/ppermute | solution.py:547
  226.8 14.6 %collective-permute-start.45 = (bf16[2,192,768]{2,1,0:T(8,128)(2,1)S(1)}, bf16[2,192,768]{2,1,0:T(8,128)(2,1)S(1)}, u32[]{:S(2)}, u32[]{:S(2)}) collective-permute-start(bf16[2,192,768]{2,1,0:T(8,128)(2,1)S(1)} %slice.616), channel_id=1, source_target_pairs={{0,2},{1,3},{2,0},{3,1},{4,6},{5,7},{6,4},{7,5},{8,10},{9,11},{10,... | collective-permute-start | bytes 1769480 | tf_op jit(solution)/shard_map/ppermute | solution.py:547
  228.1 59.0 %collective-permute-start.9 = (bf16[8,96,768]{2,1,0:T(8,128)(2,1)S(1)}, bf16[8,96,768]{2,1,0:T(8,128)(2,1)S(1)}, u32[]{:S(2)}, u32[]{:S(2)}) collective-permute-start(bf16[8,96,768]{2,1,0:T(8,128)(2,1)S(1)} %fusion.3), channel_id=1, source_target_pairs={{0,16},{8,24},{16,0},{24,8},{1,17},{9,25},{17,1},{25,9},{2,18},{10... | collective-permute-start | bytes 3538952 | tf_op jit(solution)/shard_map/ppermute | solution.py:547
  241.5 14.5 %collective-permute-start.46 = (bf16[1,192,768]{2,1,0:T(8,128)(2,1)S(1)}, bf16[1,192,768]{2,1,0:T(8,128)(2,1)S(1)}, u32[]{:S(2)}, u32[]{:S(2)}) collective-permute-start(bf16[1,192,768]{2,1,0:T(8,128)(2,1)S(1)} %slice.618), channel_id=1, source_target_pairs={{0,4},{1,5},{2,6},{3,7},{4,0},{5,1},{6,2},{7,3},{8,12},{9,13},{10,... | collective-permute-start | bytes 884744 | tf_op jit(solution)/shard_map/ppermute | solution.py:547
  244.3 43.7 %collective-permute-start.16 = (bf16[8,96,768]{2,1,0:T(8,128)(2,1)S(1)}, bf16[8,96,768]{2,1,0:T(8,128)(2,1)S(1)}, u32[]{:S(2)}, u32[]{:S(2)}) collective-permute-start(bf16[8,96,768]{2,1,0:T(8,128)(2,1)S(1)} %fusion), channel_id=1, source_target_pairs={{0,16},{8,24},{16,0},{24,8},{1,17},{9,25},{17,1},{25,9},{2,18},{10... | collective-permute-start | bytes 3538952 | tf_op jit(solution)/shard_map/ppermute | solution.py:547
  256.1 31.0 %collective-permute-start.47 = (bf16[192,768]{1,0:T(8,128)(2,1)S(1)}, bf16[192,768]{1,0:T(8,128)(2,1)S(1)}, u32[]{:S(2)}, u32[]{:S(2)}) collective-permute-start(bf16[192,768]{1,0:T(8,128)(2,1)S(1)} %bitcast.111), channel_id=1, source_target_pairs={{0,16},{8,24},{16,0},{24,8},{1,17},{9,25},{17,1},{25,9},{2,18},{10... | collective-permute-start | bytes 884744 | tf_op jit(solution)/shard_map/ppermute | solution.py:547
  277.1 39.8 %collective-permute-start.34 = (bf16[2,384,768]{2,1,0:T(8,128)(2,1)S(1)}, bf16[2,384,768]{2,1,0:T(8,128)(2,1)S(1)}, u32[]{:S(2)}, u32[]{:S(2)}) collective-permute-start(bf16[2,384,768]{2,1,0:T(8,128)(2,1)S(1)} %slice.606), channel_id=1, source_target_pairs={{0,2},{1,3},{2,0},{3,1},{4,6},{5,7},{6,4},{7,5},{8,10},{9,11},{10,... | collective-permute-start | bytes 3538952 | tf_op jit(solution)/shard_map/ppermute | solution.py:547
  287.1 3.7 collective-permute-start.48
  287.4 16.2 %collective-permute-start.10 = (bf16[4,96,768]{2,1,0:T(8,128)(2,1)S(1)}, bf16[4,96,768]{2,1,0:T(8,128)(2,1)S(1)}, u32[]{:S(2)}, u32[]{:S(2)}) collective-permute-start(bf16[4,96,768]{2,1,0:T(8,128)(2,1)S(1)} %slice.569), channel_id=1, source_target_pairs={{0,1},{1,0},{2,3},{3,2},{4,5},{5,4},{6,7},{7,6},{8,9},{9,8},{10,11... | collective-permute-start | bytes 1769480 | tf_op jit(solution)/shard_map/ppermute | solution.py:547
  288.3 27.6 %collective-permute-start.17 = (bf16[4,96,768]{2,1,0:T(8,128)(2,1)S(1)}, bf16[4,96,768]{2,1,0:T(8,128)(2,1)S(1)}, u32[]{:S(2)}, u32[]{:S(2)}) collective-permute-start(bf16[4,96,768]{2,1,0:T(8,128)(2,1)S(1)} %slice.583), channel_id=1, source_target_pairs={{0,1},{1,0},{2,3},{3,2},{4,5},{5,4},{6,7},{7,6},{8,9},{9,8},{10,11... | collective-permute-start | bytes 1769480 | tf_op jit(solution)/shard_map/ppermute | solution.py:547
  303.7 16.0 %collective-permute-start.11 = (bf16[2,96,768]{2,1,0:T(8,128)(2,1)S(1)}, bf16[2,96,768]{2,1,0:T(8,128)(2,1)S(1)}, u32[]{:S(2)}, u32[]{:S(2)}) collective-permute-start(bf16[2,96,768]{2,1,0:T(8,128)(2,1)S(1)} %slice.571), channel_id=1, source_target_pairs={{0,2},{1,3},{2,0},{3,1},{4,6},{5,7},{6,4},{7,5},{8,10},{9,11},{10,... | collective-permute-start | bytes 884744 | tf_op jit(solution)/shard_map/ppermute | solution.py:547
  316.0 15.3 %collective-permute-start.18 = (bf16[2,96,768]{2,1,0:T(8,128)(2,1)S(1)}, bf16[2,96,768]{2,1,0:T(8,128)(2,1)S(1)}, u32[]{:S(2)}, u32[]{:S(2)}) collective-permute-start(bf16[2,96,768]{2,1,0:T(8,128)(2,1)S(1)} %slice.585), channel_id=1, source_target_pairs={{0,2},{1,3},{2,0},{3,1},{4,6},{5,7},{6,4},{7,5},{8,10},{9,11},{10,... | collective-permute-start | bytes 884744 | tf_op jit(solution)/shard_map/ppermute | solution.py:547
  317.1 47.0 %collective-permute-start.35 = (bf16[1,384,768]{2,1,0:T(8,128)(2,1)S(1)}, bf16[1,384,768]{2,1,0:T(8,128)(2,1)S(1)}, u32[]{:S(2)}, u32[]{:S(2)}) collective-permute-start(bf16[1,384,768]{2,1,0:T(8,128)(2,1)S(1)} %slice.608), channel_id=1, source_target_pairs={{0,4},{1,5},{2,6},{3,7},{4,0},{5,1},{6,2},{7,3},{8,12},{9,13},{10,... | collective-permute-start | bytes 1769480 | tf_op jit(solution)/shard_map/ppermute | solution.py:547
  319.8 36.7 %collective-permute-start.12 = (bf16[1,96,768]{2,1,0:T(8,128)(2,1)S(1)}, bf16[1,96,768]{2,1,0:T(8,128)(2,1)S(1)}, u32[]{:S(2)}, u32[]{:S(2)}) collective-permute-start(bf16[1,96,768]{2,1,0:T(8,128)(2,1)S(1)} %slice.573), channel_id=1, source_target_pairs={{0,4},{1,5},{2,6},{3,7},{4,0},{5,1},{6,2},{7,3},{8,12},{9,13},{10,... | collective-permute-start | bytes 442376 | tf_op jit(solution)/shard_map/ppermute | solution.py:547
  331.3 26.8 %collective-permute-start.19 = (bf16[1,96,768]{2,1,0:T(8,128)(2,1)S(1)}, bf16[1,96,768]{2,1,0:T(8,128)(2,1)S(1)}, u32[]{:S(2)}, u32[]{:S(2)}) collective-permute-start(bf16[1,96,768]{2,1,0:T(8,128)(2,1)S(1)} %slice.587), channel_id=1, source_target_pairs={{0,4},{1,5},{2,6},{3,7},{4,0},{5,1},{6,2},{7,3},{8,12},{9,13},{10,... | collective-permute-start | bytes 442376 | tf_op jit(solution)/shard_map/ppermute | solution.py:547
  356.5 6.0 %collective-permute-start.13 = (bf16[96,768]{1,0:T(8,128)(2,1)S(1)}, bf16[96,768]{1,0:T(8,128)(2,1)S(1)}, u32[]{:S(2)}, u32[]{:S(2)}) collective-permute-start(bf16[96,768]{1,0:T(8,128)(2,1)S(1)} %bitcast.116), channel_id=1, source_target_pairs={{0,16},{8,24},{16,0},{24,8},{1,17},{9,25},{17,1},{25,9},{2,18},{10... | collective-permute-start | bytes 442376 | tf_op jit(solution)/shard_map/ppermute | solution.py:547
  358.1 6.0 %collective-permute-start.20 = (bf16[96,768]{1,0:T(8,128)(2,1)S(1)}, bf16[96,768]{1,0:T(8,128)(2,1)S(1)}, u32[]{:S(2)}, u32[]{:S(2)}) collective-permute-start(bf16[96,768]{1,0:T(8,128)(2,1)S(1)} %bitcast.115), channel_id=1, source_target_pairs={{0,16},{8,24},{16,0},{24,8},{1,17},{9,25},{17,1},{25,9},{2,18},{10... | collective-permute-start | bytes 442376 | tf_op jit(solution)/shard_map/ppermute | solution.py:547
  362.5 2.1 collective-permute-start.14
  364.1 1.6 collective-permute-start.21
  364.2 15.8 %collective-permute-start.36 = (bf16[384,768]{1,0:T(8,128)(2,1)S(1)}, bf16[384,768]{1,0:T(8,128)(2,1)S(1)}, u32[]{:S(2)}, u32[]{:S(2)}) collective-permute-start(bf16[384,768]{1,0:T(8,128)(2,1)S(1)} %bitcast.107), channel_id=1, source_target_pairs={{0,16},{8,24},{16,0},{24,8},{1,17},{9,25},{17,1},{25,9},{2,18},{10... | collective-permute-start | bytes 1769480 | tf_op jit(solution)/shard_map/ppermute | solution.py:547
  380.1 2.9 collective-permute-start.37
  (61 other events, 503.8 us)
